TPU v7x, 128 devices: a whole 4x4x4 slice. The times are simulated.
128 devices in a mesh: dp: 8 (over y, core), decode: 16 (over z, x).
Axes of the slice: x: 4, y: 4, z: 4, core: 2. Of those that a mesh axis runs over, the one named last changes fastest.
Arguments:
- unique_ids: int32 [131072], P(('dp', 'decode')), may hold values from 0 to 5592404
- hash_mult: int32 [1024], replicated, may hold values from 1 to 32748
- hash_add: int32 [1024], replicated, may hold values from 0 to 32748
- lookups: int32 [65536, 26], P(('dp', 'decode')), may hold values from 0 to 1023
- weight_in: bfloat16 [1024, 1800], P(('dp', 'decode')), may hold values from -0.1875 to 0.1875
- bias_in: float32 [1800], replicated, may hold values from -3 to 3
- weight_out: bfloat16 [1800, 128], replicated, may hold values from -0.125 to 0.125
- bias_out: float32 [128], replicated, may hold values from -3 to 3
- cotangent: bfloat16 [65536, 3328], P(('dp', 'decode')), may hold values from -0.046875 to 0.046875
Outputs:
- sample_embeddings: bfloat16 [65536, 3328], P(('dp', 'decode'))
- grad_weight_in: float32 [1024, 1800], P(('dp', 'decode'))
- grad_bias_in: float32 [1800], replicated
- grad_weight_out: float32 [1800, 128], replicated
- grad_bias_out: float32 [128], replicated
All inputs are finite; a program needn't handle non-finite values.
Results may differ from a plain program's by a relative error of at most 0.006.
Values may be sent and summed in bfloat16 or wider, within the bound.
A program may use at most 128 MiB of HBM per device.

v0:
```python
import jax
import jax.numpy as jnp
from jax import lax
from jax.sharding import PartitionSpec as P

BUCKETS = 32749


def mish_act(values):
    return values * jnp.tanh(jax.nn.softplus(values))


def mish_backward(values, upstream):
    return jax.vjp(mish_act, values)[1](upstream)[0]


def encode_ids(id_values, hash_mult, hash_add):
    reduced = id_values % BUCKETS
    codes = (hash_mult[None, :] * reduced[:, None] + hash_add[None, :]) % BUCKETS
    code_scale = 2.0 / (BUCKETS - 1)
    return (codes.astype(jnp.float32) * code_scale - 1.0).astype(jnp.bfloat16)


def per_device(
    unique_ids, hash_mult, hash_add, lookups, weight_in, bias_in, weight_out, bias_out, cotangent
):
    unique_count = unique_ids.shape[0]
    sample_count = lookups.shape[0]
    feature_count = lookups.shape[1]
    embed_width = weight_out.shape[1]
    encoded = encode_ids(unique_ids, hash_mult, hash_add)
    columns = encoded
    product = jnp.dot(
        columns,
        lax.all_gather(weight_in, ("dp", "decode"), axis=0, tiled=True),
        preferred_element_type=jnp.float32,
    )
    pre_act = product + bias_in
    hidden = mish_act(pre_act).astype(jnp.bfloat16)
    embedded = (jnp.dot(hidden, weight_out, preferred_element_type=jnp.float32) + bias_out).astype(
        jnp.bfloat16
    )
    sample_out = jnp.take(embedded, lookups.reshape(-1), axis=0).reshape(
        sample_count, feature_count * embed_width
    )
    upstream = cotangent.reshape(sample_count, feature_count, embed_width)
    half_count = feature_count // 2
    unique_index = jnp.arange(unique_count, dtype=jnp.int32)
    total = jnp.zeros((unique_count, embed_width), jnp.float32)
    for start_feature in (0, half_count):
        picked = lookups[:, start_feature : start_feature + half_count]
        one_hot = (picked[:, :, None] == unique_index[None, None, :]).astype(jnp.bfloat16)
        total = total + jnp.einsum(
            "sfu,sfe->ue",
            one_hot,
            upstream[:, start_feature : start_feature + half_count],
            preferred_element_type=jnp.float32,
        )
    d_rows = total.astype(jnp.bfloat16)
    d_hidden = lax.dot_general(
        d_rows, weight_out, (((1,), (1,)), ((), ())), preferred_element_type=jnp.float32
    )
    d_pre = mish_backward(pre_act, d_hidden).astype(jnp.bfloat16)
    local_w_out = lax.dot_general(
        hidden, d_rows, (((0,), (0,)), ((), ())), preferred_element_type=jnp.float32
    )
    local_b_in = jnp.sum(d_pre.astype(jnp.float32), axis=0)
    local_b_out = jnp.sum(d_rows.astype(jnp.float32), axis=0)
    grad_w_out, grad_b_in, grad_b_out = lax.psum(
        (local_w_out, local_b_in, local_b_out), ("dp", "decode")
    )
    columns = encoded
    grad_w_in = lax.psum_scatter(
        lax.dot_general(
            columns, d_pre, (((0,), (0,)), ((), ())), preferred_element_type=jnp.float32
        ),
        ("dp", "decode"),
        scatter_dimension=0,
        tiled=True,
    )
    return (sample_out, grad_w_in, grad_b_in, grad_w_out, grad_b_out)


def solution(mesh):
    placed = (
        P(("dp", "decode")),
        P(),
        P(),
        P(("dp", "decode"), None),
        P(("dp", "decode"), None),
        P(),
        P(),
        P(),
        P(("dp", "decode"), None),
    )
    return jax.shard_map(
        per_device,
        mesh=mesh,
        in_specs=placed,
        out_specs=(P(("dp", "decode"), None), P(("dp", "decode"), None), P(), P(), P()),
        check_vma=False,
    )
```

profile of v0, /device:TPU:1, one launch (start us, length us, event | category | flops | bytes accessed | tf_op | source)
XLA Modules:
  0.0 286.2 jit_solution(7118533448967371630)
XLA Ops:
  7.2 0.7 all-gather.2.cloned.1.call-update
  7.9 0.0 all-reduce.5.cloned.1.call-start
  8.0 5.6 %copy.23 = bf16[512,3328]{0,1:T(8,128)(2,1)} copy(bf16[512,3328]{1,0:T(8,128)(2,1)} %param.17) | data formatting | bytes 6815744 | tf_op args[8]
  13.6 6.0 %fusion.23 = f32[1024,128]{1,0:T(8,128)S(1)} fusion(bf16[512,26,128]{0,2,1:T(8,128)(2,1)} %bitcast.20, s32[512,13]{0,1:T(8,128)S(1)} %get-tuple-element.20), kind=kOutput, calls=%fused_computation.34 | convolution fusion | flops 1751646208 | bytes 2254848 | tf_op jit(solution)/shard_map/sfu,sfe->ue/dot_general | solution.py:53
  19.6 5.1 %convert_reduce_fusion.1 = (f32[128]{0:T(128)S(1)}, bf16[1024,128]{1,0:T(8,128)(2,1)S(1)}) fusion(f32[1024,128]{1,0:T(8,128)S(1)} %fusion.23, bf16[512,26,128]{0,2,1:T(8,128)(2,1)S(1)} %bitcast.21, s32[512,13]{0,1:T(8,128)S(1)} %get-tuple-element.19), kind=kOutput, calls=%fused_computation.40 | convolution fusion | flops 1752170368 | bytes 2523648 | tf_op jit(solution)/shard_map/sfu,sfe->ue/dot_general | solution.py:53
  24.7 56.4 %all-gather.2.cloned.1.call-done = bf16[1024,1800]{1,0:T(8,128)(2,1)} async-done(((bf16[8,1800]{1,0:T(8,128)(2,1)}), bf16[1024,1800]{1,0:T(8,128)(2,1)}) %all-gather.2.cloned.1.call-update) | async-done | bytes 3686416 | tf_op jit(solution)/shard_map/all_gather | solution.py:35
  81.1 12.4 %fusion.9 = (bf16[1024,1800]{0,1:T(8,128)(2,1)S(1)}, f32[1024,1800]{0,1:T(8,128)S(1)}) fusion(f32[1800]{0:T(1024)S(1)} %copy-done.5, bf16[1024,1800]{1,0:T(8,128)(2,1)} %all-gather.2.cloned.1.call-done, s32[1024]{0:T(1024)S(1)} %copy-done.6, s32[1024]{0:T(1024)S(1)} %add_select_fusion.1, s32[1024]{0:T(1024)S(1)} %copy-done.7), kind=kOutput, calls=%fused_computation.18 | convolution fusion | flops 3804045312 | bytes 14765088 | tf_op jit(solution)/shard_map/dot_general | solution.py:33
  93.5 10.5 %convert_reduce_fusion = (f32[1800]{0:T(1024)S(1)}, bf16[1024,1800]{0,1:T(8,128)(2,1)S(1)}) fusion(f32[1024,1800]{0,1:T(8,128)S(1)} %get-tuple-element.22, f32[1800]{0:T(1024)S(1)} %copy-done.5, bf16[1024,128]{1,0:T(8,128)(2,1)S(1)} %get-tuple-element.26, bf16[1800,128]{1,0:T(8,128)(2,1)S(1)} %copy-done), kind=kOutput, calls=%fused_computation.15 | convolution fusion | flops 514251008 | bytes 11796544 | tf_op jit(solution)/shard_map/dot_general | solution.py:60
  104.0 10.0 %fusion.17 = f32[1024,1800]{1,0:T(8,128)} fusion(bf16[1024,1800]{0,1:T(8,128)(2,1)S(1)} %get-tuple-element.24, s32[1024]{0:T(1024)S(1)} %copy-done.6, s32[1024]{0:T(1024)S(1)} %add_select_fusion.1, s32[1024]{0:T(1024)S(1)} %copy-done.7), kind=kOutput, calls=%fused_computation.30 | convolution fusion | flops 3787456512 | bytes 11071488 | tf_op jit(solution)/shard_map/dot_general | solution.py:74
  114.0 2.2 fusion.45
  116.2 0.1 copy.21
  116.3 0.2 reshape.61
  116.6 0.1 compare_select_fusion.3
  116.7 0.1 copy-done.8
  116.8 3.3 %fusion.35 = bf16[1024,128]{1,0:T(8,128)(2,1)S(1)} fusion(bf16[1024,1800]{0,1:T(8,128)(2,1)} %copy-done.1, bf16[1800,128]{1,0:T(8,128)(2,1)S(1)} %copy-done, f32[128]{0:T(128)S(1)} %copy-done.8), kind=kOutput, calls=%fused_computation.39 | convolution fusion | flops 472121344 | bytes 4409856 | tf_op jit(solution)/shard_map/dot_general | solution.py:40
  120.1 47.2 %gather_fusion = bf16[13312,128]{1,0:T(8,128)(2,1)} fusion(bf16[1024,128]{1,0:T(8,128)(2,1)S(1)} %fusion.35, s32[13312]{0:T(1024)S(1)} %broadcast_clamp_fusion), kind=kCustom, calls=%fused_computation | custom fusion | bytes 6868992 | tf_op jit(solution)/shard_map/jit(_take)/gather | solution.py:43
  167.4 7.5 %gather.7 = bf16[512,3328]{1,0:T(8,128)(2,1)} reshape(bf16[13312,128]{1,0:T(8,128)(2,1)} %gather_fusion) | data formatting | bytes 6815744 | tf_op jit(solution)/shard_map/jit(_take)/gather | solution.py:43
  174.8 5.5 %copy.22 = bf16[512,3328]{0,1:T(8,128)(2,1)} copy(bf16[512,3328]{1,0:T(8,128)(2,1)} %gather.7) | data formatting | bytes 6815744 | tf_op jit(solution)/shard_map/jit(_take)/gather | solution.py:43
  180.4 4.0 %bitcast_select_fusion = bf16[512,3328]{0,1:T(8,128)(2,1)} fusion(bf16[512,3328]{0,1:T(8,128)(2,1)} %copy.22, pred[512,26]{0,1:T(8,128)(4,1)S(1)} %compare_and_fusion), kind=kLoop, calls=%fused_computation.20 | loop fusion | flops 1703936 | bytes 6829056 | tf_op jit(solution)/shard_map/jit(_take)/select_n | solution.py:43
  184.4 5.6 %copy.26 = bf16[512,3328]{1,0:T(8,128)(2,1)} copy(bf16[512,3328]{0,1:T(8,128)(2,1)} %bitcast_select_fusion) | data formatting | bytes 6815744
  190.0 62.8 %all-reduce.1 = (f32[1800]{0:T(1024)}, f32[128]{0:T(128)}) all-reduce(f32[1800]{0:T(1024)S(1)} %get-tuple-element.23, f32[128]{0:T(128)S(1)} %get-tuple-element.25), channel_id=1, replica_groups=mesh['dp'=8,'decode'=16] {'dp','decode'}, use_global_device_ids=true, to_apply=%region_2.3 | all-reduce | flops 1928 | bytes 15424 | tf_op jit(solution)/shard_map/psum | solution.py:69
  252.7 23.0 %all-reduce.5.cloned.1.call-done = (f32[1024,1800]{1,0:T(8,128)}, f32[1800,128]{1,0:T(8,128)}) async-done(((f32[1024,1800]{1,0:T(8,128)}, f32[1800,128]{1,0:T(8,128)}), (f32[1024,1800]{1,0:T(8,128)}, f32[1800,128]{1,0:T(8,128)})) %all-reduce.5.cloned.1.call-update) | async-done | bytes 8294416
  275.7 1.5 constant_dynamic-slice_fusion
  277.2 2.2 copy.31
  (23 shorter events, 0.2 us)
Async XLA Ops:
  7.2 86.3 %copy-start = (bf16[1800,128]{1,0:T(8,128)(2,1)S(1)}, bf16[1800,128]{1,0:T(8,128)(2,1)}, u32[]{:S(2)}) copy-start(bf16[1800,128]{1,0:T(8,128)(2,1)} %param.15) | copy-start | bytes 1382404
  7.2 6.4 %copy-start.4 = (s32[1024]{0:T(1024)S(1)}, s32[1024]{0:T(1024)}, u32[]{:S(2)}) copy-start(s32[1024]{0:T(1024)} %param.9) | copy-start | bytes 12292
  7.2 6.4 %copy-start.3 = (s32[512,26]{0,1:T(8,128)S(1)}, s32[512,26]{0,1:T(8,128)}, u32[]{:S(2)}) copy-start(s32[512,26]{0,1:T(8,128)} %param.12) | copy-start | bytes 159748
  7.2 73.9 %all-gather.2.cloned.1.call-start = ((), (), s32[]{:S(2)}) async-start(), calls=%async_computation | async-start | bytes 3962880 | tf_op jit(solution)/shard_map/all_gather | solution.py:35
  7.9 267.8 %all-reduce.5.cloned.1.call-start = ((), (), s32[]{:S(2)}) async-start(), calls=%async_computation.1 | async-start | bytes 17571840
  13.6 6.0 %copy-start.2 = (bf16[512,3328]{0,1:T(8,128)(2,1)S(1)}, bf16[512,3328]{0,1:T(8,128)(2,1)}, u32[]{:S(2)}) copy-start(bf16[512,3328]{0,1:T(8,128)(2,1)} %copy.23) | copy-start | bytes 10223620
  19.6 61.5 %copy-start.5 = (f32[1800]{0:T(1024)S(1)}, f32[1800]{0:T(1024)}, u32[]{:S(2)}) copy-start(f32[1800]{0:T(1024)} %param.14) | copy-start | bytes 21604
  19.6 61.5 %copy-start.6 = (s32[1024]{0:T(1024)S(1)}, s32[1024]{0:T(1024)}, u32[]{:S(2)}) copy-start(s32[1024]{0:T(1024)} %param.11) | copy-start | bytes 12292
  19.6 61.5 %copy-start.7 = (s32[1024]{0:T(1024)S(1)}, s32[1024]{0:T(1024)}, u32[]{:S(2)}) copy-start(s32[1024]{0:T(1024)} %param.10) | copy-start | bytes 12292
  93.5 20.5 %copy-start.1 = (bf16[1024,1800]{0,1:T(8,128)(2,1)}, bf16[1024,1800]{0,1:T(8,128)(2,1)S(1)}, u32[]{:S(2)}) copy-start(bf16[1024,1800]{0,1:T(8,128)(2,1)S(1)} %get-tuple-element.21) | copy-start | bytes 11059204
  116.1 0.7 copy-start.8
Sparse Core Ops, SparseCore 0:
  11.0 70.0 all-gather.1
  116.3 159.4 all-reduce.4
where the time goes:
time: 287 us; the launch traced here: 286 us
  waiting for transfers between devices  80.1 us (28%)
  local copies, waits for them, and re-layouts  75.5 us (26%)
  blocking collectives  62.8 us (22%)
  matrix products  49.4 us (17%)
  between operations  14.2 us (5%)
  other arithmetic  4.15 us (1%)
    psum x1, blocking collectives, per_device(): lax.psum((local_w_out, local_b_in, local_b_out), ('dp', 'decode'))  62.8 us
    gather x3, local copies, waits for them, and re-layouts, per_device(): jnp.take(embedded, lookups.reshape(-1), axis=0)  60.2 us
    all_gather x1, waiting for transfers between devices, per_device(): lax.all_gather(weight_in, ('dp', 'decode'), axis=0, tiled=True)  56.4 us
    unnamed x3, waiting for transfers between devices  23.7 us
    unnamed x23, local copies, waits for them, and re-layouts  15 us
    dot_general x1, matrix products, per_device(): jnp.dot(columns, lax.all_gather(weight_in, ('dp', 'decode'), axis=0, tile...  12.4 us
    dot_general x2, matrix products, per_device(): jnp.einsum('sfu,sfe->ue', one_hot, upstream[:, start_feature:start_featur...  11.1 us
    dot_general x1, matrix products, per_device(): lax.dot_general(d_rows, weight_out, (((1,), (1,)), ((), ())), preferred_e...  10.5 us
  transfers between devices with their start and end apart: 2, of which 2 were waited for; matrix products, arithmetic and copies ran while one was open for 32% of the time, Pallas kernels for 0%

commit v1 on v0

v1 whole, which is shorter than its diff:
```python
import functools

import jax
import jax.numpy as jnp
from jax import lax
from jax.experimental import pallas as pl
from jax.experimental.pallas import tpu as pltpu
from jax.sharding import PartitionSpec as P

MESH = pl.DeviceIdType.MESH
BUCKETS = 32749
BF16 = jnp.bfloat16
F32 = jnp.float32
UROWS = 256


def fold(value):
    return value - (value >> 15) * BUCKETS


def last_fold(value):
    return jnp.where(value >= BUCKETS, value - BUCKETS, value)


def hashed(mult, reduced, add):
    codes = last_fold(fold(fold(mult * reduced + add)))
    return (codes.astype(F32) * (2.0 / (BUCKETS - 1)) - 1.0).astype(BF16)


def as_column(row):
    return jnp.transpose(jnp.broadcast_to(row, (128, 128)))


class Link:
    def __init__(self, send_sems, recv_sems):
        self.send_sems, self.recv_sems, self.used, self.sent = send_sems, recv_sems, 0, []

    def slot(self):
        self.used += 1
        return self.used - 1

    def copy(self, slot, src, dst, device):
        return pltpu.make_async_remote_copy(
            src_ref=src,
            dst_ref=dst,
            send_sem=self.send_sems.at[slot],
            recv_sem=self.recv_sems.at[slot],
            device_id=device,
            device_id_type=MESH,
        )

    def send(self, slot, src, dst, device):
        made = self.copy(slot, src, dst, device)
        made.start()
        self.sent.append(made)

    def finish(self):
        for made in self.sent:
            made.wait_send()


def kernel(
    dims, blocks, streams,
    par_ref, look_ref, look_t_ref, w_in_ref, b_in_ref, w_out_ref, b_out_ref, cot_hbm,
    sample_hbm, g_in_ref, g_out_ref, bias_ref,
    cot, stage, hi_b, lo_b, lo_t, enc, enc_t, w32, chip32, wg, wout, demb_acc, demb, demb_t,
    hidden, d_pre, emb_acc, table,
    a_send, a_own, a_recv, s1, r1, s2f, s2, r2, s3, r3,
    t_send, t_own, t_recv, t1f, t1, t1r, t2, t3, tf, bc, bx, by, bz,
    send_sems, recv_sems, cot_sem, out_sems,
):
    nx, ny, nz = dims
    codes = enc.shape[1]
    ids = enc.shape[0]
    samples, feats = cot.shape[0], cot.shape[1] // 128
    units = g_in_ref.shape[1]
    dp, dec = lax.axis_index("dp"), lax.axis_index("decode")
    y, core = dp // 2, dp % 2
    z, x = dec // nx, dec % nx
    other = 1 - core
    here = {"x": x, "y": y, "z": z}
    size = {"x": nx, "y": ny, "z": nz}

    def device(**moved):
        at = dict(here, core=core)
        at.update(moved)
        return (at["y"] * 2 + at["core"], at["z"] * nx + at["x"])

    def peers(axis):
        n = size[axis]
        return [((here[axis] + k + 1) % n, (here[axis] + n - k - 1) % n) for k in range(n - 1)]

    link = Link(send_sems, recv_sems)

    barrier = pltpu.get_barrier_semaphore()
    count = 1
    pl.semaphore_signal(barrier, inc=1, device_id=device(core=other), device_id_type=MESH)
    for axis in "xyz":
        for ahead, _ in peers(axis):
            pl.semaphore_signal(barrier, inc=1, device_id=device(**{axis: ahead}), device_id_type=MESH)
            count += 1
    cot_copy = pltpu.make_async_copy(cot_hbm, cot, cot_sem)
    cot_copy.start()

    w32[...] = jnp.zeros_like(w32)
    w32[:, :units] = w_in_ref[...].astype(F32)
    filled = (units // 16) * 16
    wout[filled:, :] = jnp.zeros((wout.shape[0] - filled, 128), BF16)
    wout[:filled, :] = w_out_ref[:filled, :]
    rest = jnp.concatenate([w_out_ref[filled:units, :].astype(F32), jnp.zeros((16 - units + filled, 128), F32)], axis=0)
    wout[filled : filled + 16, :] = rest.astype(BF16)

    ids_row = last_fold(fold(par_ref[0:1, :]))

    pl.semaphore_wait(barrier, count)
    pair = link.slot()
    link.send(pair, w32, chip32.at[core], device(core=other))
    chip32[core] = w32[...]

    @pl.loop(0, codes // 128)
    def _(i):
        at = pl.ds(pl.multiple_of(i * 128, 128), 128)
        mult, add = as_column(par_ref[3:4, at]), as_column(par_ref[4:5, at])
        for j in range(ids // 128):
            enc_t[at, j * 128 : (j + 1) * 128] = hashed(mult, ids_row[:, j * 128 : (j + 1) * 128], add)

    link.copy(pair, w32, chip32.at[other], device(core=other)).wait_recv()
    half = w32.shape[1] // 2
    mine = pl.ds(pl.multiple_of(core * half, 128), half)
    theirs = pl.ds(pl.multiple_of(other * half, 128), half)
    wg[x, y, z, :, mine] = chip32[:, :, mine].reshape(16, half).astype(BF16)

    def gather_slice(order, step, axis_at, columns):
        at = dict(here)
        at.update(axis_at)
        for axis in order[:step]:
            at[axis] = slice(None)
        return wg.at[at["x"], at["y"], at["z"], :, columns]

    gather_slots = {}

    def gather_send(step):
        for s, (order, start, width) in enumerate(streams):
            columns = pl.ds(pl.multiple_of(core * half + start, 128), width)
            if step == 3:
                slot = gather_slots[s, step] = link.slot()
                ref = wg.at[:, :, :, :, columns]
                link.send(slot, ref, ref, device(core=other))
                continue
            axis = order[step]
            for k, (ahead, _) in enumerate(peers(axis)):
                slot = gather_slots[s, step, k] = link.slot()
                ref = gather_slice(order, step, {}, columns)
                link.send(slot, ref, ref, device(**{axis: ahead}))

    def gather_recv(step):
        for s, (order, start, width) in enumerate(streams):
            if step == 3:
                columns = pl.ds(pl.multiple_of(other * half + start, 128), width)
                ref = wg.at[:, :, :, :, columns]
                link.copy(gather_slots[s, step], ref, ref, device(core=other)).wait_recv()
                continue
            columns = pl.ds(pl.multiple_of(core * half + start, 128), width)
            axis = order[step]
            for k, (ahead, behind) in enumerate(peers(axis)):
                ref = gather_slice(order, step, {axis: behind}, columns)
                link.copy(gather_slots[s, step, k], ref, ref, device(**{axis: ahead})).wait_recv()

    gather_send(0)

    @pl.loop(0, ids // 128)
    def _(i):
        at = pl.ds(pl.multiple_of(i * 128, 128), 128)
        reduced = as_column(last_fold(fold(par_ref[0:1, at])))
        for j in range(codes // 128):
            to = slice(j * 128, (j + 1) * 128)
            enc[at, to] = hashed(par_ref[1:2, to], reduced, par_ref[2:3, to])

    gather_recv(0)
    gather_send(1)

    look = look_ref[...]
    hi_q = (look >> 8).astype(F32).astype(BF16)
    lo_q = (look & 255).astype(F32).astype(BF16)

    @pl.loop(0, feats // 2)
    def _(i):
        at = pl.ds(pl.multiple_of(i * 256, 256), 256)
        which = (lax.broadcasted_iota(jnp.int32, (128, 256), 1) >> 7) + 2 * i
        spread = jnp.where(which == lax.broadcasted_iota(jnp.int32, (128, 256), 0), 1.0, 0.0).astype(BF16)
        hi_b[:, at] = jnp.dot(hi_q, spread, preferred_element_type=F32).astype(BF16)
        lo_b[:, at] = jnp.dot(lo_q, spread, preferred_element_type=F32).astype(BF16)

    lo_tq = (look_t_ref[...] & 255).astype(F32).astype(BF16)
    rows = lo_t.shape[0] * 16
    spread_t = jnp.where(
        (lax.broadcasted_iota(jnp.int32, (rows, 32), 0) >> 4) == lax.broadcasted_iota(jnp.int32, (rows, 32), 1), 1.0, 0.0
    ).astype(BF16)
    lo_t[...] = jnp.dot(spread_t, lo_tq, preferred_element_type=F32).astype(BF16).reshape(lo_t.shape)

    demb_acc[...] = jnp.zeros_like(demb_acc)
    cot_copy.wait()
    one, zero = jnp.array(1, BF16), jnp.array(0, BF16)

    def scatter_steps(first, last):
        @pl.loop(first, last)
        def _(i):
            iota = lax.broadcasted_iota(jnp.int32, (256, 128), 0).astype(F32).astype(BF16)
            iota = jnp.concatenate([iota] * (samples // 128), axis=1).reshape(16, 16, samples)
            left, right = [], []
            for q in range(2):
                f = 2 * i + q
                at = pl.ds(pl.multiple_of(f * 128, 128), 128)
                hit = lo_t[pl.ds(f, 1)] == iota
                left.append(jnp.where(hit, one, zero).reshape(256, samples))
                high, rows_of = hi_b[:, at], cot[:, at]
                right.append(
                    jnp.concatenate([jnp.where(high == jnp.array(h, BF16), rows_of, zero) for h in range(4)], axis=1)
                )
            demb_acc[...] += jnp.dot(
                jnp.concatenate(left, axis=1), jnp.concatenate(right, axis=0), preferred_element_type=F32
            )

    pairs = feats // 2
    scatter_steps(0, 3)
    gather_recv(1)
    gather_send(2)
    scatter_steps(3, pairs - 1)
    gather_recv(2)
    gather_send(3)
    scatter_steps(pairs - 1, pairs)

    for h in range(4):
        block = demb_acc[:, h * 128 : (h + 1) * 128].astype(BF16)
        demb[h * 256 : (h + 1) * 256, :] = block
        demb_t[:, h * 256 : (h + 1) * 256] = jnp.transpose(block.astype(F32)).astype(BF16)
    bc[core] = jnp.zeros((16, 128), F32)
    bc[core, 15:16, :] = jnp.sum(demb[...].astype(F32), axis=0, keepdims=True)
    emb_acc[...] = jnp.zeros_like(emb_acc)
    gather_recv(3)

    slots = {}

    def total(parts):
        result = parts[0]
        for part in parts[1:]:
            result = result + part
        return result

    def in_send(j):
        start, width, _ = blocks[j]
        at = pl.ds(start, width)
        slots[j, "a"] = link.slot()
        link.send(slots[j, "a"], a_send.at[:, at], a_recv.at[:, at], device(core=other))

    def first_slice(ref, axis, rank, at):
        return ref.at[rank, :, :, at] if axis == "x" else ref.at[:, rank, :, at]

    def in_first(j):
        start, width, order = blocks[j]
        at = pl.ds(start, width)
        link.copy(slots[j, "a"], a_send.at[:, at], a_recv.at[:, at], device(core=other)).wait_recv()
        summed = a_own[:, at] + a_recv[:, at].astype(F32)
        a_own[:, at] = summed
        s1[:, :, :, at] = summed.astype(BF16).reshape(nx, ny, nz * 8, width)
        axis = order[0]
        for k, (ahead, _) in enumerate(peers(axis)):
            slot = slots[j, "1", k] = link.slot()
            link.send(slot, first_slice(s1, axis, ahead, at), r1.at[k, :, :, at], device(**{axis: ahead}))

    def in_second(j):
        start, width, order = blocks[j]
        at = pl.ds(start, width)
        axis, axis2 = order[0], order[1]
        for k, (ahead, _) in enumerate(peers(axis)):
            link.copy(
                slots[j, "1", k], first_slice(s1, axis, ahead, at), r1.at[k, :, :, at], device(**{axis: ahead})
            ).wait_recv()
        n1, n2 = size[axis], size[axis2]
        step = nz * 8
        own = []
        for i in range(n2):
            cell = here["x"] * ny + i if axis == "x" else i * ny + here["y"]
            own.append(a_own[pl.ds(pl.multiple_of(cell * step, 8), step), at])
        for i in range(n2):
            summed = total([own[i]] + [r1[k, i, :, at].astype(F32) for k in range(n1 - 1)])
            s2f[i, :, at] = summed
            s2[i, :, at] = summed.astype(BF16)
        for k, (ahead, _) in enumerate(peers(axis2)):
            slot = slots[j, "2", k] = link.slot()
            link.send(slot, s2.at[ahead, :, at], r2.at[k, :, at], device(**{axis2: ahead}))

    def in_third(j):
        start, width, order = blocks[j]
        at = pl.ds(start, width)
        axis2 = order[1]
        for k, (ahead, _) in enumerate(peers(axis2)):
            link.copy(slots[j, "2", k], s2.at[ahead, :, at], r2.at[k, :, at], device(**{axis2: ahead})).wait_recv()
        summed = total([s2f[here[axis2], :, at]] + [r2[k, :, at].astype(F32) for k in range(size[axis2] - 1)])
        s3[:, :, at] = summed.reshape(nz, 8, width)
        for k, (ahead, _) in enumerate(peers("z")):
            slot = slots[j, "3", k] = link.slot()
            link.send(slot, s3.at[ahead, :, at], r3.at[k, :, at], device(z=ahead))

    def in_last(j):
        start, width, order = blocks[j]
        at = pl.ds(start, width)
        for k, (ahead, _) in enumerate(peers("z")):
            link.copy(slots[j, "3", k], s3.at[ahead, :, at], r3.at[k, :, at], device(z=ahead)).wait_recv()
        valid = min(width, units - start)
        summed = total([s3[z, :, at]] + [r3[k, :, at] for k in range(nz - 1)])
        g_in_ref[:, start : start + valid] = summed[:, :valid]

    def out_send(j):
        start, width, _ = blocks[j]
        at = pl.ds(start, width)
        slots[j, "ta"] = link.slot()
        link.send(slots[j, "ta"], t_send.at[:, at], t_recv.at[:, at], device(core=other))

    def out_first(j):
        start, width, _ = blocks[j]
        at = pl.ds(start, width)
        link.copy(slots[j, "ta"], t_send.at[:, at], t_recv.at[:, at], device(core=other)).wait_recv()
        summed = (t_own[:, at] + t_recv[:, at].astype(F32)).reshape(nx, 64 // nx, width)
        t1f[:, :, at] = summed
        t1[:, :, at] = summed.astype(BF16)
        for k, (ahead, _) in enumerate(peers("x")):
            slot = slots[j, "t1", k] = link.slot()
            link.send(slot, t1.at[ahead, :, at], t1r.at[k, :, at], device(x=ahead))

    def spread_sum(j, tag, axis, ref, at, value):
        ref[here[axis], :, at] = value.astype(ref.dtype)
        for k, (ahead, _) in enumerate(peers(axis)):
            slot = slots[j, tag, k] = link.slot()
            one_of = ref.at[here[axis], :, at]
            link.send(slot, one_of, one_of, device(**{axis: ahead}))

    def spread_wait(j, tag, axis, ref, at):
        for k, (ahead, behind) in enumerate(peers(axis)):
            one_of = ref.at[behind, :, at]
            link.copy(slots[j, tag, k], one_of, one_of, device(**{axis: ahead})).wait_recv()

    def spread_total(j, tag, axis, ref, at):
        spread_wait(j, tag, axis, ref, at)
        return total([ref[k, :, at].astype(F32) for k in range(size[axis])])

    def out_second(j):
        start, width, _ = blocks[j]
        at = pl.ds(start, width)
        for k, (ahead, _) in enumerate(peers("x")):
            link.copy(slots[j, "t1", k], t1.at[ahead, :, at], t1r.at[k, :, at], device(x=ahead)).wait_recv()
        summed = total([t1f[x, :, at]] + [t1r[k, :, at].astype(F32) for k in range(nx - 1)])
        spread_sum(j, "t2", "y", t2, at, summed)

    def out_third(j):
        start, width, _ = blocks[j]
        at = pl.ds(start, width)
        spread_sum(j, "t3", "z", t3, at, spread_total(j, "t2", "y", t2, at))

    def out_fourth(j):
        start, width, _ = blocks[j]
        at = pl.ds(start, width)
        spread_sum(j, "t4", "x", tf.at[core], at, spread_total(j, "t3", "z", t3, at))

    def out_fifth(j):
        start, width, _ = blocks[j]
        at = pl.ds(start, width)
        spread_wait(j, "t4", "x", tf.at[core], at)
        slot = slots[j, "t5"] = link.slot()
        ref = tf.at[core, :, :, at]
        link.send(slot, ref, ref, device(core=other))

    def out_last(j):
        start, width, _ = blocks[j]
        at = pl.ds(start, width)
        ref = tf.at[other, :, :, at]
        link.copy(slots[j, "t5"], ref, ref, device(core=other)).wait_recv()
        for first in range(start, start + width, 128):
            valid = min(128, units - first)
            part = tf[:, :, :, first : first + 128].reshape(128, 128)
            g_out_ref[first : first + valid, :] = jnp.transpose(part)[:valid, :]

    def bias_first():
        slots["b", "c"] = link.slot()
        link.send(slots["b", "c"], bc.at[core], bc.at[core], device(core=other))

    everything = slice(None)

    def bias_second():
        ref = bc.at[other]
        link.copy(slots["b", "c"], ref, ref, device(core=other)).wait_recv()
        spread_sum("b", "x", "x", bx, everything, bc[0] + bc[1])

    def bias_third():
        spread_sum("b", "y", "y", by, everything, spread_total("b", "x", "x", bx, everything))

    def bias_fourth():
        spread_sum("b", "z", "z", bz, everything, spread_total("b", "y", "y", by, everything))

    def bias_last():
        bias_ref[...] = spread_total("b", "z", "z", bz, everything)

    chain_in = [in_first, in_second, in_third, in_last]
    chain_out = [out_first, out_second, out_third, out_fourth, out_fifth, out_last]
    chain_bias = [bias_second, bias_third, bias_fourth, bias_last]
    pending = []

    def advance():
        for entry in list(pending):
            entry.pop(0)()
            if not entry:
                pending.remove(entry)

    for j, (start, width, _) in enumerate(blocks):
        at = slice(start, start + width)

        @pl.loop(0, ids // UROWS)
        def _(i):
            some = pl.ds(pl.multiple_of(i * UROWS, UROWS), UROWS)
            pre = jnp.dot(enc[some, :], wg[:, :, :, :, at].reshape(codes, width), preferred_element_type=F32)
            pre = pre + b_in_ref[:, at]
            grown = jnp.exp(jnp.minimum(pre, 20.0))
            up = grown * (grown + 2.0)
            inverse = 1.0 / (up + 2.0)
            active = (pre * (up * inverse)).astype(BF16)
            slope = inverse * (up + 4.0 * pre * (grown * (1.0 + grown)) * inverse)
            hidden[some, :width] = active
            d_hidden = lax.dot_general(demb[some, :], wout[at, :], (((1,), (1,)), ((), ())), preferred_element_type=F32)
            d_pre[some, :width] = (d_hidden * slope).astype(BF16)
            emb_acc[some, :] += jnp.dot(active, wout[at, :], preferred_element_type=F32)

        advance()
        grad = jnp.dot(demb_t[...], hidden[:, :width], preferred_element_type=F32)
        t_own[:, at] = jnp.where(core == 0, grad[:64], grad[64:])
        t_send[:, at] = jnp.where(core == 0, grad[64:], grad[:64]).astype(BF16)
        out_send(j)
        rows_half = codes // 2
        to_send = pl.ds(pl.multiple_of(other * rows_half, 16), rows_half)
        to_keep = pl.ds(pl.multiple_of(core * rows_half, 16), rows_half)
        a_send[:, at] = jnp.dot(enc_t[to_send, :], d_pre[:, :width], preferred_element_type=F32).astype(BF16)
        in_send(j)
        advance()
        a_own[:, at] = jnp.dot(enc_t[to_keep, :], d_pre[:, :width], preferred_element_type=F32)
        sums = jnp.dot(jnp.ones((16, ids), BF16), d_pre[:, :width], preferred_element_type=F32)
        for c in range(width // 128):
            row = start // 128 + c
            bc[core, row : row + 1, :] = sums[0:1, c * 128 : (c + 1) * 128]
        pending.append([functools.partial(step, j) for step in chain_in])
        pending.append([functools.partial(step, j) for step in chain_out])
    bias_first()
    pending.append(list(chain_bias))

    embedded = (emb_acc[...] + b_out_ref[...]).astype(BF16)
    for h in range(4):
        table[:, h * 128 : (h + 1) * 128] = embedded[h * 256 : (h + 1) * 256, :]

    out_copies = []

    def look_up(first, last, slot):
        @pl.loop(first, last)
        def _(f):
            at = pl.ds(pl.multiple_of(f * 128, 128), 128)
            lane = lax.broadcasted_iota(jnp.int32, (16, 128), 1)
            low, high = lo_b[:, at], hi_b[:, at]
            parts = []
            for c in range(2):
                iota = jnp.concatenate([(lane + 128 * c).astype(F32).astype(BF16)] * (samples // 16), axis=0)
                parts.append(jnp.where(low == iota, one, zero))
            found = jnp.dot(jnp.concatenate(parts, axis=1), table[...], preferred_element_type=F32).astype(BF16)
            result = found[:, 384:512]
            for h in (2, 1, 0):
                result = jnp.where(high == jnp.array(h, BF16), found[:, h * 128 : (h + 1) * 128], result)
            stage[:, at] = result

        at = pl.ds(first * 128, (last - first) * 128)
        made = pltpu.make_async_copy(stage.at[:, at], sample_hbm.at[:, at], out_sems.at[slot])
        made.start()
        out_copies.append(made)

    cuts = [round(feats * i / 6) for i in range(7)]
    for i in range(6):
        look_up(cuts[i], cuts[i + 1], i)
        advance()
    while pending:
        advance()
    link.finish()
    for made in out_copies:
        made.wait()


def per_device(dims, unique_ids, hash_mult, hash_add, lookups, weight_in, bias_in, weight_out, bias_out, cotangent):
    nx, ny, nz = dims
    ids, codes = unique_ids.shape[0], hash_mult.shape[0]
    samples, feats = lookups.shape
    units, emb = weight_out.shape
    padded = -(-units // 128) * 128
    wide = -(-units // 256) * 256
    each = codes // (2 * nx * ny * nz)

    def reorder(values, to):
        return values.reshape(ny, 2, nz, nx, each).transpose(to).reshape(1, codes)

    by_chip, by_core = (3, 0, 2, 1, 4), (1, 3, 0, 2, 4)
    par = jnp.concatenate(
        [
            unique_ids.reshape(1, ids),
            *[
                jnp.pad(reorder(v, to), ((0, 0), (0, ids - codes)))
                for to in (by_chip, by_core)
                for v in (hash_mult, hash_add)
            ],
            jnp.zeros((3, ids), jnp.int32),
        ],
        axis=0,
    )
    look = jnp.pad(lookups, ((0, 0), (0, 128 - feats)))
    look_t = jnp.pad(lookups.T, ((0, 32 - feats), (0, 0)))
    bias = jnp.pad(bias_in, (0, padded - units)).reshape(1, padded)

    blocks, start = [], 0
    while start < padded:
        width = min(512, padded - start)
        blocks.append((start, width, ("x", "y") if len(blocks) % 2 == 0 else ("y", "x")))
        start += width
    half = wide // 2
    third = -(-half // 384) * 128
    streams, start = [], 0
    for order in ("xyz", "yzx", "zxy"):
        width = min(third, half - start)
        streams.append((order, start, width))
        start += width

    VMEM = pltpu.VMEM
    rows = codes // 2
    scratch = [
        VMEM((samples, feats * emb), BF16),
        VMEM((samples, feats * emb), BF16),
        VMEM((samples, feats * emb), BF16),
        VMEM((samples, feats * emb), BF16),
        VMEM((feats, 16, samples), BF16),
        VMEM((ids, codes), BF16),
        VMEM((codes, ids), BF16),
        VMEM((8, wide), F32),
        VMEM((2, 8, wide), F32),
        VMEM((nx, ny, nz, 16, wide), BF16),
        VMEM((padded, emb), BF16),
        VMEM((256, 4 * emb), F32),
        VMEM((ids, emb), BF16),
        VMEM((emb, ids), BF16),
        VMEM((ids, 512), BF16),
        VMEM((ids, 512), BF16),
        VMEM((ids, emb), F32),
        VMEM((256, 4 * emb), BF16),
        VMEM((rows, padded), BF16),
        VMEM((rows, padded), F32),
        VMEM((rows, padded), BF16),
        VMEM((nx, ny, nz * 8, padded), BF16),
        VMEM((3, 4, nz * 8, padded), BF16),
        VMEM((4, nz * 8, padded), F32),
        VMEM((4, nz * 8, padded), BF16),
        VMEM((3, nz * 8, padded), BF16),
        VMEM((nz, 8, padded), F32),
        VMEM((3, 8, padded), F32),
        VMEM((64, padded), BF16),
        VMEM((64, padded), F32),
        VMEM((64, padded), BF16),
        VMEM((nx, 64 // nx, padded), F32),
        VMEM((nx, 64 // nx, padded), BF16),
        VMEM((3, 64 // nx, padded), BF16),
        VMEM((ny, 64 // nx, padded), BF16),
        VMEM((nz, 64 // nx, padded), BF16),
        VMEM((2, nx, 64 // nx, padded), F32),
        VMEM((2, 16, 128), F32),
        VMEM((nx, 16, 128), F32),
        VMEM((ny, 16, 128), F32),
        VMEM((nz, 16, 128), F32),
        pltpu.SemaphoreType.DMA((160,)),
        pltpu.SemaphoreType.DMA((160,)),
        pltpu.SemaphoreType.DMA,
        pltpu.SemaphoreType.DMA((6,)),
    ]
    whole = pl.BlockSpec(memory_space=pltpu.VMEM)
    remote = pl.BlockSpec(memory_space=pl.ANY)
    sample_out, grad_in, grad_out, biases = pl.pallas_call(
        functools.partial(kernel, dims, blocks, streams),
        out_shape=(
            jax.ShapeDtypeStruct((samples, feats * emb), BF16),
            jax.ShapeDtypeStruct((8, units), F32),
            jax.ShapeDtypeStruct((units, emb), F32),
            jax.ShapeDtypeStruct((16, 128), F32),
        ),
        in_specs=[whole] * 7 + [remote],
        out_specs=(remote, whole, whole, whole),
        scratch_shapes=scratch,
        compiler_params=pltpu.CompilerParams(
            collective_id=0, has_side_effects=True, vmem_limit_bytes=60 * 1024 * 1024
        ),
    )(par, look, look_t, weight_in, bias, weight_out, bias_out.reshape(1, emb), cotangent)
    flat = biases.reshape(2048)
    return sample_out, grad_in, flat[:units], grad_out, flat[1920:2048]


def solution(mesh):
    nx = {4: 2, 16: 4}[mesh.shape["decode"]]
    dims = (nx, mesh.shape["dp"] // 2, mesh.shape["decode"] // nx)
    both = ("dp", "decode")
    return jax.shard_map(
        functools.partial(per_device, dims),
        mesh=mesh,
        in_specs=(P(both), P(), P(), P(both, None), P(both, None), P(), P(), P(), P(both, None)),
        out_specs=(P(both, None), P(both, None), P(), P(), P()),
        check_vma=False,
    )
```

time: 287 us -> 121 us (0.42)
  Pallas kernels: 0 us -> 105 us
  waiting for transfers between devices: 80.1 us -> 0 us
  blocking collectives: 62.8 us -> 0 us
  local copies, waits for them, and re-layouts: 75.5 us -> 15.4 us
  matrix products: 49.4 us -> 0 us
  between operations: 14.2 us -> 0.72 us
  other arithmetic: 4.15 us -> 0 us
    pallas_call x0 -> x1, Pallas kernels: none -> 105 us  [per_device(): pl.pallas_call(functools.partial(kernel, dims, blocks, streams), out_shap...]
    psum x1 -> x0, blocking collectives: 62.8 us -> none  [per_device(): lax.psum((local_w_out, local_b_in, local_b_out), ('dp', 'decode'))]
    gather x3 -> x0, local copies, waits for them, and re-layouts: 60.2 us -> none  [per_device(): jnp.take(embedded, lookups.reshape(-1), axis=0)]
    all_gather x1 -> x0, waiting for transfers between devices: 56.4 us -> none  [per_device(): lax.all_gather(weight_in, ('dp', 'decode'), axis=0, tiled=True)]
    dot_general x7 -> x0, matrix products: 49.4 us -> none  [the longest x1 12.4 us: per_device(): jnp.dot(columns, lax.all_gather(weight_in, ('dp', 'decode'), axis=0, tile...]
    unnamed x3 -> x0, waiting for transfers between devices: 23.7 us -> none
    unnamed x23 -> x11, local copies, waits for them, and re-layouts: 15 us -> 7.15 us
    select_n x3 -> x0, other arithmetic: 4.11 us -> none  [the longest x2 4.1 us: per_device(): jnp.take(embedded, lookups.reshape(-1), axis=0)]
  transfers between devices with their start and end apart: 2 -> 0, of which waited for: 2 -> 0; matrix products, arithmetic and copies ran while one was open for 32% -> 0% of each run, Pallas kernels for 0% -> 0%
where the time goes in v1:
time: 121 us
  Pallas kernels  105 us (87%)
  local copies, waits for them, and re-layouts  15.4 us (13%)
    pallas_call x1, Pallas kernels, per_device(): pl.pallas_call(functools.partial(kernel, dims, blocks, streams), out_shap...  105 us
    unnamed x11, local copies, waits for them, and re-layouts  7.15 us

profile of v1, /device:TPU:1, one launch (start us, length us, event | category | flops | bytes accessed | tf_op | source)
XLA Modules:
  0.0 121.0 jit_solution(7597458176498082981)
XLA Ops:
  0.6 0.7 pad.14
  1.3 0.6 reshape.50.b_in_ref
  1.9 0.8 reshape.44
  2.7 0.8 reshape.46
  3.6 0.1 reshape.47
  3.8 0.1 reshape.49
  3.9 0.1 reshape.45
  4.1 0.1 reshape.48
  4.2 1.3 %concatenate.3.par_ref = s32[8,1024]{1,0:T(8,128)} concatenate(s32[1,1024]{1,0:T(1,128)} %bitcast.17, s32[1,1024]{1,0:T(1,128)S(1)} %reshape.45, s32[1,1024]{1,0:T(1,128)S(1)} %reshape.47, s32[1,1024]{1,0:T(1,128)S(1)} %reshape.48, s32[1,1024]{1,0:T(1,128)S(1)} %reshape.49, s32[3,1024]{1,0:T(4,128)S(1)} %broadcast_in_dim.3), dimensions={0} | concatenate | bytes 65536 | tf_op jit(solution)/shard_map/concatenate | solution.py:504
  5.6 1.5 %pad.13.look_t_ref = s32[32,512]{1,0:T(8,128)} pad(s32[26,512]{1,0:T(8,128)} %bitcast.15, s32[]{:T(128)} %constant.1.clone.1), padding=0_6x0_0 | pad | bytes 118788 | tf_op jit(solution)/shard_map/jit(_pad)/pad | solution.py:517
  7.0 1.0 copy.21
  8.0 0.7 pad.12.look_ref
  8.7 104.9 %shard_map.128 = (bf16[512,3328]{1,0:T(8,128)(2,1)}, f32[8,1800]{1,0:T(8,128)}, f32[1800,128]{1,0:T(8,128)}, f32[16,128]{1,0:T(8,128)}) custom-call(s32[8,1024]{1,0:T(8,128)} %concatenate.3.par_ref, s32[512,128]{1,0:T(8,128)} %pad.12.look_ref, s32[32,512]{1,0:T(8,128)} %pad.13.look_t_ref, bf16[8,1800]{1,0:T(8,128)(2,1)} %w_in_ref.1, ...), custom_call_target="tpu_custom_call" | custom-call | tf_op jit(solution)/shard_map/pallas_call | solution.py:584
  113.7 1.2 slice_bitcast_fusion
  114.8 0.0 copy-start.1
  114.8 0.0 copy-start.2
  114.9 0.0 copy-start
  114.9 4.0 %copy.26 = bf16[512,3328]{1,0:T(8,128)(2,1)} copy(bf16[512,3328]{1,0:T(8,128)(2,1)} %get-tuple-element.18) | data formatting | bytes 6815744
  118.9 0.0 copy-done.1
  118.9 0.6 copy.27
  119.5 0.0 copy-done.2
  119.5 0.6 copy.28
  120.1 0.0 copy-done
  120.1 0.9 copy.29
  (5 shorter events, 0.1 us)
Async XLA Ops:
  114.8 4.0 %copy-start.1 = (f32[8,1800]{1,0:T(8,128)S(1)}, f32[8,1800]{1,0:T(8,128)}, u32[]{:S(2)}) copy-start(f32[8,1800]{1,0:T(8,128)} %get-tuple-element.19) | copy-start | bytes 172804
  114.8 4.6 %copy-start.2 = (f32[16,128]{1,0:T(8,128)S(1)}, f32[16,128]{1,0:T(8,128)}, u32[]{:S(2)}) copy-start(f32[16,128]{1,0:T(8,128)} %get-tuple-element.11) | copy-start | bytes 24580
  114.9 5.2 %copy-start = (f32[1800,128]{1,0:T(8,128)S(1)}, f32[1800,128]{1,0:T(8,128)}, u32[]{:S(2)}) copy-start(f32[1800,128]{1,0:T(8,128)} %get-tuple-element.21) | copy-start | bytes 2764804

commit v2 on v1

--- a/solution.py
+++ b/solution.py
@@ -60,12 +60,12 @@
 
 
 def kernel(
-    dims, blocks, streams,
-    par_ref, look_ref, look_t_ref, w_in_ref, b_in_ref, w_out_ref, b_out_ref, cot_hbm,
+    dims, blocks, groups, rounds,
+    ids_ref, mult_ref, add_ref, look_t_ref, w_in_ref, b_in_ref, w_out_ref, b_out_ref, cot_hbm,
     sample_hbm, g_in_ref, g_out_ref, bias_ref,
-    cot, stage, hi_b, lo_b, lo_t, enc, enc_t, w32, chip32, wg, wout, demb_acc, demb, demb_t,
+    red, mult_f, add_f, bias, cot, stage, hi_b, lo_b, lo_t, enc, enc_t, w32, chip32, wg, wout, demb_acc, demb, demb_t,
     hidden, d_pre, emb_acc, table,
-    a_send, a_own, a_recv, s1, r1, s2f, s2, r2, s3, r3,
+    a_send, a_own, a_recv, s1f, s1, r1, s2f, s2, r2, s3, r3,
     t_send, t_own, t_recv, t1f, t1, t1r, t2, t3, tf, bc, bx, by, bz,
     send_sems, recv_sems, cot_sem, out_sems,
 ):
@@ -110,7 +110,16 @@
     rest = jnp.concatenate([w_out_ref[filled:units, :].astype(F32), jnp.zeros((16 - units + filled, 128), F32)], axis=0)
     wout[filled : filled + 16, :] = rest.astype(BF16)
 
-    ids_row = last_fold(fold(par_ref[0:1, :]))
+    bias[...] = jnp.zeros_like(bias)
+    bias[0:1, :units] = b_in_ref[...].reshape(1, units)
+    red[...] = last_fold(fold(ids_ref[...]))
+
+    for given, ordered in ((mult_ref, mult_f), (add_ref, add_f)):
+        for i in range(ny):
+            parts = [as_column(given[2 * i + c : 2 * i + c + 1, :]).reshape(16, 1, 8, 128) for c in range(2)]
+            mixed = jnp.concatenate(parts, axis=1).reshape(256, 128)
+            for c in range(2):
+                ordered[2 * i + c : 2 * i + c + 1, :] = jnp.transpose(mixed[c * 128 : (c + 1) * 128, :])[0:1, :]
 
     pl.semaphore_wait(barrier, count)
     pair = link.slot()
@@ -120,66 +129,71 @@
     @pl.loop(0, codes // 128)
     def _(i):
         at = pl.ds(pl.multiple_of(i * 128, 128), 128)
-        mult, add = as_column(par_ref[3:4, at]), as_column(par_ref[4:5, at])
+        row = pl.ds((i % ny) * 2 + i // ny, 1)
+        mult, add = as_column(mult_ref[row, :]), as_column(add_ref[row, :])
         for j in range(ids // 128):
-            enc_t[at, j * 128 : (j + 1) * 128] = hashed(mult, ids_row[:, j * 128 : (j + 1) * 128], add)
+            enc_t[at, j * 128 : (j + 1) * 128] = hashed(mult, red[j : j + 1, :], add)
 
     link.copy(pair, w32, chip32.at[other], device(core=other)).wait_recv()
-    half = w32.shape[1] // 2
-    mine = pl.ds(pl.multiple_of(core * half, 128), half)
-    theirs = pl.ds(pl.multiple_of(other * half, 128), half)
-    wg[x, y, z, :, mine] = chip32[:, :, mine].reshape(16, half).astype(BF16)
+    for start, width, _ in rounds:
+        columns = pl.ds(pl.multiple_of(start + core * width, 128), width)
+        wg[y, z, x, :, columns] = chip32[:, :, columns].reshape(16, width).astype(BF16)
 
     def gather_slice(order, step, axis_at, columns):
         at = dict(here)
         at.update(axis_at)
         for axis in order[:step]:
             at[axis] = slice(None)
-        return wg.at[at["x"], at["y"], at["z"], :, columns]
+        return wg.at[at["y"], at["z"], at["x"], :, columns]
 
     gather_slots = {}
 
-    def gather_send(step):
-        for s, (order, start, width) in enumerate(streams):
-            columns = pl.ds(pl.multiple_of(core * half + start, 128), width)
-            if step == 3:
-                slot = gather_slots[s, step] = link.slot()
-                ref = wg.at[:, :, :, :, columns]
-                link.send(slot, ref, ref, device(core=other))
-                continue
-            axis = order[step]
-            for k, (ahead, _) in enumerate(peers(axis)):
-                slot = gather_slots[s, step, k] = link.slot()
+    def gather_send(r, step):
+        first, width, streams = rounds[r]
+        if step == 3:
+            columns = pl.ds(pl.multiple_of(first + core * width, 128), width)
+            slot = gather_slots[r] = link.slot()
+            ref = wg.at[:, :, :, :, columns]
+            link.send(slot, ref, ref, device(core=other))
+            return
+        for s, (order, start, wide) in enumerate(streams):
+            columns = pl.ds(pl.multiple_of(first + core * width + start, 128), wide)
+            for k, (ahead, _) in enumerate(peers(order[step])):
+                slot = gather_slots[r, s, step, k] = link.slot()
                 ref = gather_slice(order, step, {}, columns)
-                link.send(slot, ref, ref, device(**{axis: ahead}))
-
-    def gather_recv(step):
-        for s, (order, start, width) in enumerate(streams):
-            if step == 3:
-                columns = pl.ds(pl.multiple_of(other * half + start, 128), width)
-                ref = wg.at[:, :, :, :, columns]
-                link.copy(gather_slots[s, step], ref, ref, device(core=other)).wait_recv()
-                continue
-            columns = pl.ds(pl.multiple_of(core * half + start, 128), width)
-            axis = order[step]
-            for k, (ahead, behind) in enumerate(peers(axis)):
-                ref = gather_slice(order, step, {axis: behind}, columns)
-                link.copy(gather_slots[s, step, k], ref, ref, device(**{axis: ahead})).wait_recv()
-
-    gather_send(0)
+                link.send(slot, ref, ref, device(**{order[step]: ahead}))
+
+    def gather_recv(r, step):
+        first, width, streams = rounds[r]
+        if step == 3:
+            columns = pl.ds(pl.multiple_of(first + other * width, 128), width)
+            ref = wg.at[:, :, :, :, columns]
+            link.copy(gather_slots[r], ref, ref, device(core=other)).wait_recv()
+            return
+        for s, (order, start, wide) in enumerate(streams):
+            columns = pl.ds(pl.multiple_of(first + core * width + start, 128), wide)
+            for k, (ahead, behind) in enumerate(peers(order[step])):
+                ref = gather_slice(order, step, {order[step]: behind}, columns)
+                link.copy(gather_slots[r, s, step, k], ref, ref, device(**{order[step]: ahead})).wait_recv()
+
+    gather_send(0, 0)
+    gather_send(1, 0)
 
     @pl.loop(0, ids // 128)
     def _(i):
         at = pl.ds(pl.multiple_of(i * 128, 128), 128)
-        reduced = as_column(last_fold(fold(par_ref[0:1, at])))
+        reduced = as_column(red[pl.ds(i, 1), :])
         for j in range(codes // 128):
             to = slice(j * 128, (j + 1) * 128)
-            enc[at, to] = hashed(par_ref[1:2, to], reduced, par_ref[2:3, to])
-
-    gather_recv(0)
-    gather_send(1)
-
-    look = look_ref[...]
+            enc[at, to] = hashed(mult_f[j : j + 1, :], reduced, add_f[j : j + 1, :])
+
+    gather_recv(0, 0)
+    gather_send(0, 1)
+    gather_recv(1, 0)
+    gather_send(1, 1)
+
+    look_t = jnp.concatenate([look_t_ref[...], jnp.zeros((128 - feats, samples), jnp.int32)], axis=0)
+    look = jnp.transpose(look_t)
     hi_q = (look >> 8).astype(F32).astype(BF16)
     lo_q = (look & 255).astype(F32).astype(BF16)
 
@@ -191,7 +205,7 @@
         hi_b[:, at] = jnp.dot(hi_q, spread, preferred_element_type=F32).astype(BF16)
         lo_b[:, at] = jnp.dot(lo_q, spread, preferred_element_type=F32).astype(BF16)
 
-    lo_tq = (look_t_ref[...] & 255).astype(F32).astype(BF16)
+    lo_tq = (look_t[:32, :] & 255).astype(F32).astype(BF16)
     rows = lo_t.shape[0] * 16
     spread_t = jnp.where(
         (lax.broadcasted_iota(jnp.int32, (rows, 32), 0) >> 4) == lax.broadcasted_iota(jnp.int32, (rows, 32), 1), 1.0, 0.0
@@ -222,13 +236,15 @@
             )
 
     pairs = feats // 2
-    scatter_steps(0, 3)
-    gather_recv(1)
-    gather_send(2)
-    scatter_steps(3, pairs - 1)
-    gather_recv(2)
-    gather_send(3)
-    scatter_steps(pairs - 1, pairs)
+    gather_recv(0, 1)
+    gather_send(0, 2)
+    scatter_steps(0, 5)
+    gather_recv(1, 1)
+    gather_send(1, 2)
+    scatter_steps(5, pairs - 2)
+    gather_recv(0, 2)
+    gather_send(0, 3)
+    scatter_steps(pairs - 2, pairs)
 
     for h in range(4):
         block = demb_acc[:, h * 128 : (h + 1) * 128].astype(BF16)
@@ -237,7 +253,7 @@
     bc[core] = jnp.zeros((16, 128), F32)
     bc[core, 15:16, :] = jnp.sum(demb[...].astype(F32), axis=0, keepdims=True)
     emb_acc[...] = jnp.zeros_like(emb_acc)
-    gather_recv(3)
+    gather_recv(0, 3)
 
     slots = {}
 
@@ -253,72 +269,76 @@
         slots[j, "a"] = link.slot()
         link.send(slots[j, "a"], a_send.at[:, at], a_recv.at[:, at], device(core=other))
 
-    def first_slice(ref, axis, rank, at):
-        return ref.at[rank, :, :, at] if axis == "x" else ref.at[:, rank, :, at]
+    dims_of = ("y", "z", "x")
 
     def in_first(j):
-        start, width, order = blocks[j]
+        start, width, stripes = blocks[j]
         at = pl.ds(start, width)
         link.copy(slots[j, "a"], a_send.at[:, at], a_recv.at[:, at], device(core=other)).wait_recv()
-        summed = a_own[:, at] + a_recv[:, at].astype(F32)
-        a_own[:, at] = summed
-        s1[:, :, :, at] = summed.astype(BF16).reshape(nx, ny, nz * 8, width)
-        axis = order[0]
-        for k, (ahead, _) in enumerate(peers(axis)):
-            slot = slots[j, "1", k] = link.slot()
-            link.send(slot, first_slice(s1, axis, ahead, at), r1.at[k, :, :, at], device(**{axis: ahead}))
+        for first, wide, order in stripes:
+            at = slice(first, first + wide)
+            summed = (a_own[:, at] + a_recv[:, at].astype(F32)).reshape(ny, nz, nx, 8, wide)
+            axis = dims_of.index(order[0])
+            for i in range(size[order[0]]):
+                part = lax.index_in_dim(summed, i, axis, keepdims=False).reshape(-1, wide)
+                s1f[i, :, at] = part
+                s1[i, :, at] = part.astype(BF16)
+            at = pl.ds(first, wide)
+            for k, (ahead, _) in enumerate(peers(order[0])):
+                slot = slots[first, "1", k] = link.slot()
+                link.send(slot, s1.at[ahead, :, at], r1.at[k, :, at], device(**{order[0]: ahead}))
 
     def in_second(j):
-        start, width, order = blocks[j]
-        at = pl.ds(start, width)
-        axis, axis2 = order[0], order[1]
-        for k, (ahead, _) in enumerate(peers(axis)):
-            link.copy(
-                slots[j, "1", k], first_slice(s1, axis, ahead, at), r1.at[k, :, :, at], device(**{axis: ahead})
-            ).wait_recv()
-        n1, n2 = size[axis], size[axis2]
-        step = nz * 8
-        own = []
-        for i in range(n2):
-            cell = here["x"] * ny + i if axis == "x" else i * ny + here["y"]
-            own.append(a_own[pl.ds(pl.multiple_of(cell * step, 8), step), at])
-        for i in range(n2):
-            summed = total([own[i]] + [r1[k, i, :, at].astype(F32) for k in range(n1 - 1)])
-            s2f[i, :, at] = summed
-            s2[i, :, at] = summed.astype(BF16)
-        for k, (ahead, _) in enumerate(peers(axis2)):
-            slot = slots[j, "2", k] = link.slot()
-            link.send(slot, s2.at[ahead, :, at], r2.at[k, :, at], device(**{axis2: ahead}))
+        for first, wide, order in blocks[j][2]:
+            at = pl.ds(first, wide)
+            for k, (ahead, _) in enumerate(peers(order[0])):
+                link.copy(
+                    slots[first, "1", k], s1.at[ahead, :, at], r1.at[k, :, at], device(**{order[0]: ahead})
+                ).wait_recv()
+            summed = total([s1f[here[order[0]], :, at]] + [r1[k, :, at].astype(F32) for k in range(size[order[0]] - 1)])
+            left = [axis for axis in dims_of if axis != order[0]]
+            summed = summed.reshape(size[left[0]], size[left[1]], 8, wide)
+            axis = left.index(order[1])
+            for i in range(size[order[1]]):
+                part = lax.index_in_dim(summed, i, axis, keepdims=False).reshape(-1, wide)
+                s2f[i, :, at] = part
+                s2[i, :, at] = part.astype(BF16)
+            for k, (ahead, _) in enumerate(peers(order[1])):
+                slot = slots[first, "2", k] = link.slot()
+                link.send(slot, s2.at[ahead, :, at], r2.at[k, :, at], device(**{order[1]: ahead}))
 
     def in_third(j):
-        start, width, order = blocks[j]
-        at = pl.ds(start, width)
-        axis2 = order[1]
-        for k, (ahead, _) in enumerate(peers(axis2)):
-            link.copy(slots[j, "2", k], s2.at[ahead, :, at], r2.at[k, :, at], device(**{axis2: ahead})).wait_recv()
-        summed = total([s2f[here[axis2], :, at]] + [r2[k, :, at].astype(F32) for k in range(size[axis2] - 1)])
-        s3[:, :, at] = summed.reshape(nz, 8, width)
-        for k, (ahead, _) in enumerate(peers("z")):
-            slot = slots[j, "3", k] = link.slot()
-            link.send(slot, s3.at[ahead, :, at], r3.at[k, :, at], device(z=ahead))
+        for first, wide, order in blocks[j][2]:
+            at = pl.ds(first, wide)
+            for k, (ahead, _) in enumerate(peers(order[1])):
+                link.copy(
+                    slots[first, "2", k], s2.at[ahead, :, at], r2.at[k, :, at], device(**{order[1]: ahead})
+                ).wait_recv()
+            summed = total([s2f[here[order[1]], :, at]] + [r2[k, :, at].astype(F32) for k in range(size[order[1]] - 1)])
+            s3[:, :, at] = summed.reshape(size[order[2]], 8, wide)
+            for k, (ahead, _) in enumerate(peers(order[2])):
+                slot = slots[first, "3", k] = link.slot()
+                link.send(slot, s3.at[ahead, :, at], r3.at[k, :, at], device(**{order[2]: ahead}))
 
     def in_last(j):
-        start, width, order = blocks[j]
-        at = pl.ds(start, width)
-        for k, (ahead, _) in enumerate(peers("z")):
-            link.copy(slots[j, "3", k], s3.at[ahead, :, at], r3.at[k, :, at], device(z=ahead)).wait_recv()
-        valid = min(width, units - start)
-        summed = total([s3[z, :, at]] + [r3[k, :, at] for k in range(nz - 1)])
-        g_in_ref[:, start : start + valid] = summed[:, :valid]
+        for first, wide, order in blocks[j][2]:
+            at = pl.ds(first, wide)
+            for k, (ahead, _) in enumerate(peers(order[2])):
+                link.copy(
+                    slots[first, "3", k], s3.at[ahead, :, at], r3.at[k, :, at], device(**{order[2]: ahead})
+                ).wait_recv()
+            valid = min(wide, units - first)
+            summed = total([s3[here[order[2]], :, at]] + [r3[k, :, at] for k in range(size[order[2]] - 1)])
+            g_in_ref[:, first : first + valid] = summed[:, :valid]
 
     def out_send(j):
-        start, width, _ = blocks[j]
+        start, width = groups[j]
         at = pl.ds(start, width)
         slots[j, "ta"] = link.slot()
         link.send(slots[j, "ta"], t_send.at[:, at], t_recv.at[:, at], device(core=other))
 
     def out_first(j):
-        start, width, _ = blocks[j]
+        start, width = groups[j]
         at = pl.ds(start, width)
         link.copy(slots[j, "ta"], t_send.at[:, at], t_recv.at[:, at], device(core=other)).wait_recv()
         summed = (t_own[:, at] + t_recv[:, at].astype(F32)).reshape(nx, 64 // nx, width)
@@ -345,7 +365,7 @@
         return total([ref[k, :, at].astype(F32) for k in range(size[axis])])
 
     def out_second(j):
-        start, width, _ = blocks[j]
+        start, width = groups[j]
         at = pl.ds(start, width)
         for k, (ahead, _) in enumerate(peers("x")):
             link.copy(slots[j, "t1", k], t1.at[ahead, :, at], t1r.at[k, :, at], device(x=ahead)).wait_recv()
@@ -353,17 +373,17 @@
         spread_sum(j, "t2", "y", t2, at, summed)
 
     def out_third(j):
-        start, width, _ = blocks[j]
+        start, width = groups[j]
         at = pl.ds(start, width)
         spread_sum(j, "t3", "z", t3, at, spread_total(j, "t2", "y", t2, at))
 
     def out_fourth(j):
-        start, width, _ = blocks[j]
+        start, width = groups[j]
         at = pl.ds(start, width)
         spread_sum(j, "t4", "x", tf.at[core], at, spread_total(j, "t3", "z", t3, at))
 
     def out_fifth(j):
-        start, width, _ = blocks[j]
+        start, width = groups[j]
         at = pl.ds(start, width)
         spread_wait(j, "t4", "x", tf.at[core], at)
         slot = slots[j, "t5"] = link.slot()
@@ -371,7 +391,7 @@
         link.send(slot, ref, ref, device(core=other))
 
     def out_last(j):
-        start, width, _ = blocks[j]
+        start, width = groups[j]
         at = pl.ds(start, width)
         ref = tf.at[other, :, :, at]
         link.copy(slots[j, "t5"], ref, ref, device(core=other)).wait_recv()
@@ -400,25 +420,37 @@
     def bias_last():
         bias_ref[...] = spread_total("b", "z", "z", bz, everything)
 
-    chain_in = [in_first, in_second, in_third, in_last]
-    chain_out = [out_first, out_second, out_third, out_fourth, out_fifth, out_last]
-    chain_bias = [bias_second, bias_third, bias_fourth, bias_last]
-    pending = []
-
-    def advance():
-        for entry in list(pending):
-            entry.pop(0)()
-            if not entry:
-                pending.remove(entry)
-
-    for j, (start, width, _) in enumerate(blocks):
-        at = slice(start, start + width)
-
-        @pl.loop(0, ids // UROWS)
+    points = {
+        (0, 0): [(gather_recv, 1, 2), (gather_send, 1, 3)],
+        (0, 2): [(gather_recv, 1, 3)],
+        (1, 0): [(in_first, 0)],
+        (2, 0): [(in_first, 1), (in_second, 0), (out_first, 0)],
+        (2, 1): [(out_second, 0)],
+        (2, 2): [(in_third, 0)],
+        (3, 0): [(in_first, 2), (in_second, 1), (out_first, 1), (out_third, 0)],
+        (3, 1): [(in_last, 0), (out_second, 1)],
+        (3, 2): [(in_third, 1), (out_fourth, 0)],
+        (4, 0): [(in_first, 3), (out_first, 2), (bias_second,), (in_second, 2), (out_third, 1), (out_fifth, 0)],
+        (4, 1): [(out_second, 2), (bias_third,), (in_last, 1), (out_last, 0)],
+        (4, 2): [(in_second, 3), (in_third, 2), (out_fourth, 1)],
+        (4, 3): [(out_third, 2), (bias_fourth,)],
+        (4, 4): [(in_third, 3), (in_last, 2), (out_fifth, 1)],
+        (4, 5): [(out_fourth, 2), (bias_last,), (out_last, 1)],
+        (4, 6): [(out_fifth, 2), (in_last, 3), (out_last, 2)],
+    }
+
+    def advance(*point):
+        for step, *which in points.pop(point, ()):
+            step(*which)
+
+    def forward_backward(at, width, part):
+        steps = ids // UROWS // 2
+
+        @pl.loop(part * steps, (part + 1) * steps)
         def _(i):
             some = pl.ds(pl.multiple_of(i * UROWS, UROWS), UROWS)
             pre = jnp.dot(enc[some, :], wg[:, :, :, :, at].reshape(codes, width), preferred_element_type=F32)
-            pre = pre + b_in_ref[:, at]
+            pre = pre + bias[0:1, at]
             grown = jnp.exp(jnp.minimum(pre, 20.0))
             up = grown * (grown + 2.0)
             inverse = 1.0 / (up + 2.0)
@@ -429,26 +461,30 @@
             d_pre[some, :width] = (d_hidden * slope).astype(BF16)
             emb_acc[some, :] += jnp.dot(active, wout[at, :], preferred_element_type=F32)
 
-        advance()
+    for j, (start, width, _) in enumerate(blocks):
+        at = slice(start, start + width)
+
+        for part in range(2):
+            forward_backward(at, width, part)
+            advance(j, part)
         grad = jnp.dot(demb_t[...], hidden[:, :width], preferred_element_type=F32)
         t_own[:, at] = jnp.where(core == 0, grad[:64], grad[64:])
         t_send[:, at] = jnp.where(core == 0, grad[64:], grad[:64]).astype(BF16)
-        out_send(j)
+        for g, (first, wide) in enumerate(groups):
+            if start + width == first + wide:
+                out_send(g)
         rows_half = codes // 2
         to_send = pl.ds(pl.multiple_of(other * rows_half, 16), rows_half)
         to_keep = pl.ds(pl.multiple_of(core * rows_half, 16), rows_half)
         a_send[:, at] = jnp.dot(enc_t[to_send, :], d_pre[:, :width], preferred_element_type=F32).astype(BF16)
         in_send(j)
-        advance()
+        advance(j, 2)
         a_own[:, at] = jnp.dot(enc_t[to_keep, :], d_pre[:, :width], preferred_element_type=F32)
         sums = jnp.dot(jnp.ones((16, ids), BF16), d_pre[:, :width], preferred_element_type=F32)
         for c in range(width // 128):
             row = start // 128 + c
             bc[core, row : row + 1, :] = sums[0:1, c * 128 : (c + 1) * 128]
-        pending.append([functools.partial(step, j) for step in chain_in])
-        pending.append([functools.partial(step, j) for step in chain_out])
     bias_first()
-    pending.append(list(chain_bias))
 
     embedded = (emb_acc[...] + b_out_ref[...]).astype(BF16)
     for h in range(4):
@@ -477,12 +513,12 @@
         made.start()
         out_copies.append(made)
 
-    cuts = [round(feats * i / 6) for i in range(7)]
+    cuts = [0, 5, 9, 13, 17, 21, 26]
     for i in range(6):
         look_up(cuts[i], cuts[i + 1], i)
-        advance()
-    while pending:
-        advance()
+        advance(4, i)
+    advance(4, 6)
+    assert not points
     link.finish()
     for made in out_copies:
         made.wait()
@@ -495,44 +531,31 @@
     units, emb = weight_out.shape
     padded = -(-units // 128) * 128
     wide = -(-units // 256) * 256
-    each = codes // (2 * nx * ny * nz)
-
-    def reorder(values, to):
-        return values.reshape(ny, 2, nz, nx, each).transpose(to).reshape(1, codes)
-
-    by_chip, by_core = (3, 0, 2, 1, 4), (1, 3, 0, 2, 4)
-    par = jnp.concatenate(
-        [
-            unique_ids.reshape(1, ids),
-            *[
-                jnp.pad(reorder(v, to), ((0, 0), (0, ids - codes)))
-                for to in (by_chip, by_core)
-                for v in (hash_mult, hash_add)
-            ],
-            jnp.zeros((3, ids), jnp.int32),
-        ],
-        axis=0,
-    )
-    look = jnp.pad(lookups, ((0, 0), (0, 128 - feats)))
-    look_t = jnp.pad(lookups.T, ((0, 32 - feats), (0, 0)))
-    bias = jnp.pad(bias_in, (0, padded - units)).reshape(1, padded)
-
+    orders = ("xyz", "yzx", "zxy")
     blocks, start = [], 0
     while start < padded:
         width = min(512, padded - start)
-        blocks.append((start, width, ("x", "y") if len(blocks) % 2 == 0 else ("y", "x")))
+        stripes, first = [], start
+        for i in range(3):
+            order = orders[(i + len(blocks)) % 3]
+            each = 128 * (width // 384) + (128 if i < width // 128 % 3 else 0)
+            stripes.append((first, each, order))
+            first += each
+        blocks.append((start, width, stripes))
         start += width
-    half = wide // 2
-    third = -(-half // 384) * 128
-    streams, start = [], 0
-    for order in ("xyz", "yzx", "zxy"):
-        width = min(third, half - start)
-        streams.append((order, start, width))
-        start += width
+    groups = [(0, 1024), (1024, 512), (1536, padded - 1536)]
+    rounds = [
+        (0, 384, (("xyz", 0, 128), ("yzx", 128, 128), ("zxy", 256, 128))),
+        (768, 640, (("xyz", 0, 256), ("yzx", 256, 256), ("zxy", 512, 128))),
+    ]
 
     VMEM = pltpu.VMEM
     rows = codes // 2
     scratch = [
+        VMEM((8, 128), jnp.int32),
+        VMEM((8, 128), jnp.int32),
+        VMEM((8, 128), jnp.int32),
+        VMEM((8, padded), F32),
         VMEM((samples, feats * emb), BF16),
         VMEM((samples, feats * emb), BF16),
         VMEM((samples, feats * emb), BF16),
@@ -542,7 +565,7 @@
         VMEM((codes, ids), BF16),
         VMEM((8, wide), F32),
         VMEM((2, 8, wide), F32),
-        VMEM((nx, ny, nz, 16, wide), BF16),
+        VMEM((ny, nz, nx, 16, wide), BF16),
         VMEM((padded, emb), BF16),
         VMEM((256, 4 * emb), F32),
         VMEM((ids, emb), BF16),
@@ -554,12 +577,13 @@
         VMEM((rows, padded), BF16),
         VMEM((rows, padded), F32),
         VMEM((rows, padded), BF16),
-        VMEM((nx, ny, nz * 8, padded), BF16),
-        VMEM((3, 4, nz * 8, padded), BF16),
-        VMEM((4, nz * 8, padded), F32),
-        VMEM((4, nz * 8, padded), BF16),
-        VMEM((3, nz * 8, padded), BF16),
-        VMEM((nz, 8, padded), F32),
+        VMEM((4, rows // 4, padded), F32),
+        VMEM((4, rows // 4, padded), BF16),
+        VMEM((3, rows // 4, padded), BF16),
+        VMEM((4, rows // 16, padded), F32),
+        VMEM((4, rows // 16, padded), BF16),
+        VMEM((3, rows // 16, padded), BF16),
+        VMEM((4, 8, padded), F32),
         VMEM((3, 8, padded), F32),
         VMEM((64, padded), BF16),
         VMEM((64, padded), F32),
@@ -574,28 +598,31 @@
         VMEM((nx, 16, 128), F32),
         VMEM((ny, 16, 128), F32),
         VMEM((nz, 16, 128), F32),
-        pltpu.SemaphoreType.DMA((160,)),
-        pltpu.SemaphoreType.DMA((160,)),
+        pltpu.SemaphoreType.DMA((260,)),
+        pltpu.SemaphoreType.DMA((260,)),
         pltpu.SemaphoreType.DMA,
         pltpu.SemaphoreType.DMA((6,)),
     ]
     whole = pl.BlockSpec(memory_space=pltpu.VMEM)
     remote = pl.BlockSpec(memory_space=pl.ANY)
     sample_out, grad_in, grad_out, biases = pl.pallas_call(
-        functools.partial(kernel, dims, blocks, streams),
+        functools.partial(kernel, dims, blocks, groups, rounds),
         out_shape=(
             jax.ShapeDtypeStruct((samples, feats * emb), BF16),
             jax.ShapeDtypeStruct((8, units), F32),
             jax.ShapeDtypeStruct((units, emb), F32),
             jax.ShapeDtypeStruct((16, 128), F32),
         ),
-        in_specs=[whole] * 7 + [remote],
+        in_specs=[whole] * 8 + [remote],
         out_specs=(remote, whole, whole, whole),
         scratch_shapes=scratch,
         compiler_params=pltpu.CompilerParams(
             collective_id=0, has_side_effects=True, vmem_limit_bytes=60 * 1024 * 1024
         ),
-    )(par, look, look_t, weight_in, bias, weight_out, bias_out.reshape(1, emb), cotangent)
+    )(
+        unique_ids.reshape(8, 128), hash_mult.reshape(8, 128), hash_add.reshape(8, 128), lookups.T,
+        weight_in, bias_in, weight_out, bias_out.reshape(1, emb), cotangent,
+    )
     flat = biases.reshape(2048)
     return sample_out, grad_in, flat[:units], grad_out, flat[1920:2048]
 

time: 121 us -> 91.4 us (0.76)
  Pallas kernels: 105 us -> 83.2 us
  local copies, waits for them, and re-layouts: 15.4 us -> 7.37 us
    pallas_call x1, Pallas kernels: 105 us -> 83.2 us  [per_device(): pl.pallas_call(functools.partial(kernel, dims, blocks, groups, rounds), o...]
    pad x3 -> x0, local copies, waits for them, and re-layouts: 2.9 us -> none  [the longest x1 1.47 us: per_device(): look_t = jnp.pad(lookups.T, ((0, 32 - feats), (0, 0)))]
    reshape x7 -> x0, local copies, waits for them, and re-layouts: 2.7 us -> none  [the longest x6 2.1 us: reorder(): return values.reshape(ny, 2, nz, nx, each).transpose(to).reshape(1, codes)]
    concatenate x1 -> x0, local copies, waits for them, and re-layouts: 1.34 us -> none  [per_device(): jnp.concatenate([unique_ids.reshape(1, ids), *[jnp.pad(reorder(v, to), ((...]
    unnamed x11 -> x10, local copies, waits for them, and re-layouts: 7.15 us -> 6.17 us
where the time goes in v2:
time: 91.4 us; the launch traced here: 91.2 us
  Pallas kernels  83.2 us (91%)
  local copies, waits for them, and re-layouts  7.37 us (8%)
    pallas_call x1, Pallas kernels, per_device(): pl.pallas_call(functools.partial(kernel, dims, blocks, groups, rounds), o...  83.2 us
    unnamed x10, local copies, waits for them, and re-layouts  6.17 us

profile of v2, /device:TPU:1, one launch (start us, length us, event | category | flops | bytes accessed | tf_op | source)
XLA Modules:
  0.0 91.2 jit_solution(13877221238643098633)
XLA Ops:
  0.6 83.2 %shard_map.128 = (bf16[512,3328]{1,0:T(8,128)(2,1)}, f32[8,1800]{1,0:T(8,128)}, f32[1800,128]{1,0:T(8,128)}, f32[16,128]{1,0:T(8,128)}) custom-call(s32[8,128]{1,0:T(8,128)} %bitcast.11, s32[8,128]{1,0:T(8,128)} %bitcast.12, s32[8,128]{1,0:T(8,128)} %bitcast.13, s32[26,512]{1,0:T(8,128)} %bitcast.9, bf16[8,1800]{1,0:T(8,128)(2,1)} %w_in_ref.1, ...), custom_call_target="tpu_custom_call" | custom-call | tf_op jit(solution)/shard_map/pallas_call | solution.py:608
  83.9 1.2 %slice_bitcast_fusion = f32[128]{0:T(128)} fusion(f32[16,128]{1,0:T(8,128)} %get-tuple-element.11), kind=kLoop, calls=%fused_computation | loop fusion | bytes 1024 | tf_op jit(solution)/shard_map/slice | solution.py:627
  85.1 0.0 copy-start.1
  85.1 0.0 copy-start.2
  85.1 0.0 copy-start
  85.1 4.0 %copy.18 = bf16[512,3328]{1,0:T(8,128)(2,1)} copy(bf16[512,3328]{1,0:T(8,128)(2,1)} %get-tuple-element.18) | data formatting | bytes 6815744
  89.1 0.0 copy-done.1
  89.1 0.6 copy.19
  89.7 0.0 copy-done.2
  89.7 0.6 copy.20
  90.3 0.0 copy-done
  90.3 0.9 %copy.21 = f32[1800,128]{1,0:T(8,128)} copy(f32[1800,128]{1,0:T(8,128)S(1)} %copy-done) | data formatting | bytes 1843200
Async XLA Ops:
  85.1 4.0 %copy-start.1 = (f32[8,1800]{1,0:T(8,128)S(1)}, f32[8,1800]{1,0:T(8,128)}, u32[]{:S(2)}) copy-start(f32[8,1800]{1,0:T(8,128)} %get-tuple-element.19) | copy-start | bytes 172804
  85.1 4.6 %copy-start.2 = (f32[16,128]{1,0:T(8,128)S(1)}, f32[16,128]{1,0:T(8,128)}, u32[]{:S(2)}) copy-start(f32[16,128]{1,0:T(8,128)} %get-tuple-element.11) | copy-start | bytes 24580
  85.1 5.2 %copy-start = (f32[1800,128]{1,0:T(8,128)S(1)}, f32[1800,128]{1,0:T(8,128)}, u32[]{:S(2)}) copy-start(f32[1800,128]{1,0:T(8,128)} %get-tuple-element.21) | copy-start | bytes 2764804

commit v3 on v2

--- a/solution.py
+++ b/solution.py
@@ -11,7 +11,7 @@
 BUCKETS = 32749
 BF16 = jnp.bfloat16
 F32 = jnp.float32
-UROWS = 256
+UROWS = 512
 
 
 def fold(value):
@@ -424,19 +424,21 @@
         (0, 0): [(gather_recv, 1, 2), (gather_send, 1, 3)],
         (0, 2): [(gather_recv, 1, 3)],
         (1, 0): [(in_first, 0)],
-        (2, 0): [(in_first, 1), (in_second, 0), (out_first, 0)],
-        (2, 1): [(out_second, 0)],
-        (2, 2): [(in_third, 0)],
-        (3, 0): [(in_first, 2), (in_second, 1), (out_first, 1), (out_third, 0)],
-        (3, 1): [(in_last, 0), (out_second, 1)],
-        (3, 2): [(in_third, 1), (out_fourth, 0)],
-        (4, 0): [(in_first, 3), (out_first, 2), (bias_second,), (in_second, 2), (out_third, 1), (out_fifth, 0)],
-        (4, 1): [(out_second, 2), (bias_third,), (in_last, 1), (out_last, 0)],
-        (4, 2): [(in_second, 3), (in_third, 2), (out_fourth, 1)],
-        (4, 3): [(out_third, 2), (bias_fourth,)],
-        (4, 4): [(in_third, 3), (in_last, 2), (out_fifth, 1)],
-        (4, 5): [(out_fourth, 2), (bias_last,), (out_last, 1)],
-        (4, 6): [(out_fifth, 2), (in_last, 3), (out_last, 2)],
+        (2, 0): [(in_first, 1), (out_first, 0)],
+        (2, 1): [(in_second, 0)],
+        (3, 0): [(in_first, 2), (out_first, 1), (out_second, 0), (in_third, 0)],
+        (3, 1): [(in_second, 1)],
+        (4, 3): [(in_first, 3), (out_first, 2), (bias_second,), (out_second, 1), (out_third, 0), (in_last, 0)],
+        (4, 7): [(in_second, 2), (in_third, 1)],
+        (4, 12): [(out_second, 2), (bias_third,), (out_third, 1), (out_fourth, 0)],
+        (4, 14): [(in_second, 3)],
+        (4, 16): [(in_third, 2), (in_last, 1)],
+        (4, 21): [(out_third, 2), (bias_fourth,), (out_fourth, 1), (out_fifth, 0)],
+        (4, 23): [(in_third, 3)],
+        (4, 26): [
+            (in_last, 2), (out_last, 0), (out_fourth, 2), (bias_last,), (out_fifth, 1),
+            (in_last, 3), (out_last, 1), (out_fifth, 2), (out_last, 2),
+        ],
     }
 
     def advance(*point):
@@ -513,14 +515,35 @@
         made.start()
         out_copies.append(made)
 
-    cuts = [0, 5, 9, 13, 17, 21, 26]
-    for i in range(6):
+    cuts = [0] + [at for part, at in points if part == 4]
+    for i in range(len(cuts) - 1):
         look_up(cuts[i], cuts[i + 1], i)
-        advance(4, i)
-    advance(4, 6)
+        advance(4, cuts[i + 1])
     assert not points
     link.finish()
     for made in out_copies:
+        made.wait()
+
+
+def deliver(sample, g_in, g_out, biases, sample_to, g_in_to, g_out_to, b_in_to, b_out_to, held, held_in, held_out, sems):
+    parts = 8
+    rows = sample.shape[0] // parts
+    cuts = [pl.ds(i * rows, rows) for i in range(parts)]
+    moves = [(sample.at[cut], held.at[cut], sample_to.at[cut]) for cut in cuts]
+    moves += [(g_in, held_in, g_in_to), (g_out, held_out, g_out_to)]
+    reads = [pltpu.make_async_copy(source, via, sems.at[0, i]) for i, (source, via, _) in enumerate(moves)]
+    writes = [pltpu.make_async_copy(via, to, sems.at[1, i]) for i, (_, via, to) in enumerate(moves)]
+    for made in reads:
+        made.start()
+    units = b_in_to.shape[0]
+    for i in range(-(-units // 128)):
+        wide = min(128, units - i * 128)
+        b_in_to[i * 128 : i * 128 + wide] = biases[i, :wide]
+    b_out_to[...] = biases[15, :]
+    for read, write in zip(reads, writes):
+        read.wait()
+        write.start()
+    for made in writes:
         made.wait()
 
 
@@ -601,7 +624,7 @@
         pltpu.SemaphoreType.DMA((260,)),
         pltpu.SemaphoreType.DMA((260,)),
         pltpu.SemaphoreType.DMA,
-        pltpu.SemaphoreType.DMA((6,)),
+        pltpu.SemaphoreType.DMA((8,)),
     ]
     whole = pl.BlockSpec(memory_space=pltpu.VMEM)
     remote = pl.BlockSpec(memory_space=pl.ANY)
@@ -623,8 +646,26 @@
         unique_ids.reshape(8, 128), hash_mult.reshape(8, 128), hash_add.reshape(8, 128), lookups.T,
         weight_in, bias_in, weight_out, bias_out.reshape(1, emb), cotangent,
     )
-    flat = biases.reshape(2048)
-    return sample_out, grad_in, flat[:units], grad_out, flat[1920:2048]
+    sample_out, grad_in, grad_out, grad_b_in, grad_b_out = pl.pallas_call(
+        deliver,
+        out_shape=(
+            jax.ShapeDtypeStruct((samples, feats * emb), BF16),
+            jax.ShapeDtypeStruct((8, units), F32),
+            jax.ShapeDtypeStruct((units, emb), F32),
+            jax.ShapeDtypeStruct((units,), F32),
+            jax.ShapeDtypeStruct((emb,), F32),
+        ),
+        in_specs=[remote, remote, remote, whole],
+        out_specs=(remote, remote, remote, whole, whole),
+        scratch_shapes=[
+            VMEM((samples, feats * emb), BF16),
+            VMEM((8, units), F32),
+            VMEM((units, emb), F32),
+            pltpu.SemaphoreType.DMA((2, 10)),
+        ],
+        compiler_params=pltpu.CompilerParams(vmem_limit_bytes=16 * 1024 * 1024),
+    )(sample_out, grad_in, grad_out, biases)
+    return sample_out, grad_in, grad_b_in, grad_out, grad_b_out
 
 
 def solution(mesh):

time: 91.4 us -> 85.1 us (0.931)
  Pallas kernels: 83.2 us -> 79.3 us
  local copies, waits for them, and re-layouts: 7.37 us -> 4.66 us
    pallas_call x1, Pallas kernels: 83.2 us -> 74.4 us  [per_device(): pl.pallas_call(functools.partial(kernel, dims, blocks, groups, rounds), o...]
    pallas_call x0 -> x1, Pallas kernels: none -> 4.97 us  [per_device(): pl.pallas_call(deliver, out_shape=(jax.ShapeDtypeStruct((samples, feats *...]
    unnamed x10 -> x8, local copies, waits for them, and re-layouts: 6.17 us -> 4.66 us
    slice x1 -> x0, local copies, waits for them, and re-layouts: 1.2 us -> none  [per_device(): return (sample_out, grad_in, flat[:units], grad_out, flat[1920:2048])]
where the time goes in v3:
time: 85.1 us; the launch traced here: 84.8 us
  Pallas kernels  79.3 us (93%)
  local copies, waits for them, and re-layouts  4.66 us (5%)
    pallas_call x1, Pallas kernels, per_device(): pl.pallas_call(functools.partial(kernel, dims, blocks, groups, rounds), o...  74.4 us
    pallas_call x1, Pallas kernels, per_device(): pl.pallas_call(deliver, out_shape=(jax.ShapeDtypeStruct((samples, feats *...  4.97 us
    unnamed x8, local copies, waits for them, and re-layouts  4.66 us

profile of v3, /device:TPU:1, one launch (start us, length us, event | category | flops | bytes accessed | tf_op | source)
XLA Modules:
  0.0 84.8 jit_solution(4121864594657501797)
XLA Ops:
  0.6 74.4 %shard_map.128 = (bf16[512,3328]{1,0:T(8,128)(2,1)}, f32[8,1800]{1,0:T(8,128)}, f32[1800,128]{1,0:T(8,128)}, f32[16,128]{1,0:T(8,128)}) custom-call(s32[8,128]{1,0:T(8,128)} %bitcast.6, s32[8,128]{1,0:T(8,128)} %bitcast.7, s32[8,128]{1,0:T(8,128)} %bitcast.8, s32[26,512]{1,0:T(8,128)} %bitcast.5, bf16[8,1800]{1,0:T(8,128)(2,1)} %w_in_ref.1, f32[1800]{0:T(1024)} %b_in_ref.1, ...), custom_call_target="tpu_custom_call" | custom-call | tf_op jit(solution)/shard_map/pallas_call | solution.py:631
  75.0 0.0 copy-start
  75.0 2.0 %copy-done = bf16[512,3328]{1,0:T(8,128)(2,1)S(1)} copy-done((bf16[512,3328]{1,0:T(8,128)(2,1)S(1)}, bf16[512,3328]{1,0:T(8,128)(2,1)}, u32[]{:S(2)}) %copy-start) | copy-done | bytes 3407896
  77.0 0.0 copy-start.1
  77.0 1.2 %copy-done.1 = f32[1800,128]{1,0:T(8,128)S(1)} copy-done((f32[1800,128]{1,0:T(8,128)S(1)}, f32[1800,128]{1,0:T(8,128)}, u32[]{:S(2)}) %copy-start.1) | copy-done | bytes 921624
  78.2 0.0 copy-start.2
  78.2 0.8 copy-done.2
  79.0 0.0 copy-start.3
  79.0 0.7 copy-done.3
  79.7 5.0 %shard_map.129 = (bf16[512,3328]{1,0:T(8,128)(2,1)}, f32[8,1800]{1,0:T(8,128)}, f32[1800,128]{1,0:T(8,128)}, f32[1800]{0:T(1024)}, f32[128]{0:T(128)}) custom-call(bf16[512,3328]{1,0:T(8,128)(2,1)S(1)} %copy-done, f32[8,1800]{1,0:T(8,128)S(1)} %copy-done.2, f32[1800,128]{1,0:T(8,128)S(1)} %copy-done.1, f32[16,128]{1,0:T(8,128)S(1)} %copy-done.3), custom_call_target="tpu_custom_call" | custom-call | tf_op jit(solution)/shard_map/pallas_call | solution.py:649
Async XLA Ops:
  75.0 2.0 %copy-start = (bf16[512,3328]{1,0:T(8,128)(2,1)S(1)}, bf16[512,3328]{1,0:T(8,128)(2,1)}, u32[]{:S(2)}) copy-start(bf16[512,3328]{1,0:T(8,128)(2,1)} %get-tuple-element.14.sample) | copy-start | bytes 10223620
  77.0 1.2 %copy-start.1 = (f32[1800,128]{1,0:T(8,128)S(1)}, f32[1800,128]{1,0:T(8,128)}, u32[]{:S(2)}) copy-start(f32[1800,128]{1,0:T(8,128)} %get-tuple-element.16.g_out) | copy-start | bytes 2764804
  78.2 0.8 copy-start.2
  79.0 0.7 copy-start.3

commit v4 on v3

--- a/solution.py
+++ b/solution.py
@@ -61,13 +61,14 @@
 
 def kernel(
     dims, blocks, groups, rounds,
-    ids_ref, mult_ref, add_ref, look_t_ref, w_in_ref, b_in_ref, w_out_ref, b_out_ref, cot_hbm,
-    sample_hbm, g_in_ref, g_out_ref, bias_ref,
+    ids_hbm, mult_hbm, add_hbm, look_t_hbm, b_in_hbm, w_out_hbm, b_out_hbm, cot_hbm, w_in_ref,
+    sample_hbm, g_in_hbm, g_out_hbm, bias_hbm,
+    ids_ref, mult_ref, add_ref, look_t_ref, b_in_ref, w_out_ref, b_out_ref, g_in_ref, g_out_ref, bias_ref,
     red, mult_f, add_f, bias, cot, stage, hi_b, lo_b, lo_t, enc, enc_t, w32, chip32, wg, wout, demb_acc, demb, demb_t,
     hidden, d_pre, emb_acc, table,
     a_send, a_own, a_recv, s1f, s1, r1, s2f, s2, r2, s3, r3,
     t_send, t_own, t_recv, t1f, t1, t1r, t2, t3, tf, bc, bx, by, bz,
-    send_sems, recv_sems, cot_sem, out_sems,
+    send_sems, recv_sems, in_sems, out_sems,
 ):
     nx, ny, nz = dims
     codes = enc.shape[1]
@@ -91,6 +92,12 @@
         return [((here[axis] + k + 1) % n, (here[axis] + n - k - 1) % n) for k in range(n - 1)]
 
     link = Link(send_sems, recv_sems)
+    given = (mult_hbm, add_hbm, ids_hbm, w_out_hbm, b_in_hbm, b_out_hbm, look_t_hbm, cot_hbm)
+    kept = (mult_ref, add_ref, ids_ref, w_out_ref, b_in_ref, b_out_ref, look_t_ref, cot)
+    fetches = [pltpu.make_async_copy(source, to, in_sems.at[i]) for i, (source, to) in enumerate(zip(given, kept))]
+    for made in fetches:
+        made.start()
+    cot_copy = fetches[-1]
 
     barrier = pltpu.get_barrier_semaphore()
     count = 1
@@ -99,19 +106,11 @@
         for ahead, _ in peers(axis):
             pl.semaphore_signal(barrier, inc=1, device_id=device(**{axis: ahead}), device_id_type=MESH)
             count += 1
-    cot_copy = pltpu.make_async_copy(cot_hbm, cot, cot_sem)
-    cot_copy.start()
 
     w32[...] = jnp.zeros_like(w32)
     w32[:, :units] = w_in_ref[...].astype(F32)
-    filled = (units // 16) * 16
-    wout[filled:, :] = jnp.zeros((wout.shape[0] - filled, 128), BF16)
-    wout[:filled, :] = w_out_ref[:filled, :]
-    rest = jnp.concatenate([w_out_ref[filled:units, :].astype(F32), jnp.zeros((16 - units + filled, 128), F32)], axis=0)
-    wout[filled : filled + 16, :] = rest.astype(BF16)
-
-    bias[...] = jnp.zeros_like(bias)
-    bias[0:1, :units] = b_in_ref[...].reshape(1, units)
+    for made in fetches[:3]:
+        made.wait()
     red[...] = last_fold(fold(ids_ref[...]))
 
     for given, ordered in ((mult_ref, mult_f), (add_ref, add_f)):
@@ -125,6 +124,16 @@
     pair = link.slot()
     link.send(pair, w32, chip32.at[core], device(core=other))
     chip32[core] = w32[...]
+    for made in fetches[3:-1]:
+        made.wait()
+    bias[...] = jnp.zeros_like(bias)
+    bias[0:1, :units] = b_in_ref[...].reshape(1, units)
+    filled = (units // 16) * 16
+    wout[filled:, :] = jnp.zeros((wout.shape[0] - filled, 128), BF16)
+    wout[:filled, :] = w_out_ref[:filled, :]
+    rest = jnp.concatenate([w_out_ref[filled:units, :].astype(F32), jnp.zeros((16 - units + filled, 128), F32)], axis=0)
+    wout[filled : filled + 16, :] = rest.astype(BF16)
+
 
     @pl.loop(0, codes // 128)
     def _(i):
@@ -390,6 +399,13 @@
         ref = tf.at[core, :, :, at]
         link.send(slot, ref, ref, device(core=other))
 
+    result_copies = []
+
+    def deliver_rows(first, count, slot):
+        made = pltpu.make_async_copy(g_out_ref.at[pl.ds(first, count)], g_out_hbm.at[pl.ds(first, count)], out_sems.at[slot])
+        made.start()
+        result_copies.append(made)
+
     def out_last(j):
         start, width = groups[j]
         at = pl.ds(start, width)
@@ -399,6 +415,7 @@
             valid = min(128, units - first)
             part = tf[:, :, :, first : first + 128].reshape(128, 128)
             g_out_ref[first : first + valid, :] = jnp.transpose(part)[:valid, :]
+        deliver_rows(start, min(width, units - start), 8 + j)
 
     def bias_first():
         slots["b", "c"] = link.slot()
@@ -419,6 +436,9 @@
 
     def bias_last():
         bias_ref[...] = spread_total("b", "z", "z", bz, everything)
+        made = pltpu.make_async_copy(bias_ref, bias_hbm, out_sems.at[11])
+        made.start()
+        result_copies.append(made)
 
     points = {
         (0, 0): [(gather_recv, 1, 2), (gather_send, 1, 3)],
@@ -520,26 +540,38 @@
         look_up(cuts[i], cuts[i + 1], i)
         advance(4, cuts[i + 1])
     assert not points
+    made = pltpu.make_async_copy(g_in_ref, g_in_hbm, out_sems.at[7])
+    made.start()
+    result_copies.append(made)
     link.finish()
-    for made in out_copies:
+    for made in out_copies + result_copies:
         made.wait()
 
 
-def deliver(sample, g_in, g_out, biases, sample_to, g_in_to, g_out_to, b_in_to, b_out_to, held, held_in, held_out, sems):
+def deliver(
+    sample, g_in, g_out, biases, sample_to, g_in_to, g_out_to, b_in_to, b_out_to,
+    held, held_in, held_out, held_bias, held_b_in, held_b_out, sems,
+):
     parts = 8
     rows = sample.shape[0] // parts
     cuts = [pl.ds(i * rows, rows) for i in range(parts)]
-    moves = [(sample.at[cut], held.at[cut], sample_to.at[cut]) for cut in cuts]
-    moves += [(g_in, held_in, g_in_to), (g_out, held_out, g_out_to)]
+    moves = [(g_out, held_out, g_out_to), (g_in, held_in, g_in_to)]
+    moves += [(sample.at[cut], held.at[cut], sample_to.at[cut]) for cut in cuts]
+    fetch = pltpu.make_async_copy(biases, held_bias, sems.at[0, 10])
+    fetch.start()
     reads = [pltpu.make_async_copy(source, via, sems.at[0, i]) for i, (source, via, _) in enumerate(moves)]
     writes = [pltpu.make_async_copy(via, to, sems.at[1, i]) for i, (_, via, to) in enumerate(moves)]
     for made in reads:
         made.start()
     units = b_in_to.shape[0]
+    fetch.wait()
     for i in range(-(-units // 128)):
         wide = min(128, units - i * 128)
-        b_in_to[i * 128 : i * 128 + wide] = biases[i, :wide]
-    b_out_to[...] = biases[15, :]
+        held_b_in[i * 128 : i * 128 + wide] = held_bias[i, :wide]
+    held_b_out[...] = held_bias[15, :]
+    for i, (via, to) in enumerate(((held_b_in, b_in_to), (held_b_out, b_out_to))):
+        writes.append(pltpu.make_async_copy(via, to, sems.at[1, 10 + i]))
+        writes[-1].start()
     for read, write in zip(reads, writes):
         read.wait()
         write.start()
@@ -575,6 +607,16 @@
     VMEM = pltpu.VMEM
     rows = codes // 2
     scratch = [
+        VMEM((8, 128), jnp.int32),
+        VMEM((8, 128), jnp.int32),
+        VMEM((8, 128), jnp.int32),
+        VMEM((feats, samples), jnp.int32),
+        VMEM((units,), F32),
+        VMEM((units, emb), BF16),
+        VMEM((1, emb), F32),
+        VMEM((8, units), F32),
+        VMEM((units, emb), F32),
+        VMEM((16, 128), F32),
         VMEM((8, 128), jnp.int32),
         VMEM((8, 128), jnp.int32),
         VMEM((8, 128), jnp.int32),
@@ -623,8 +665,8 @@
         VMEM((nz, 16, 128), F32),
         pltpu.SemaphoreType.DMA((260,)),
         pltpu.SemaphoreType.DMA((260,)),
-        pltpu.SemaphoreType.DMA,
         pltpu.SemaphoreType.DMA((8,)),
+        pltpu.SemaphoreType.DMA((12,)),
     ]
     whole = pl.BlockSpec(memory_space=pltpu.VMEM)
     remote = pl.BlockSpec(memory_space=pl.ANY)
@@ -636,15 +678,15 @@
             jax.ShapeDtypeStruct((units, emb), F32),
             jax.ShapeDtypeStruct((16, 128), F32),
         ),
-        in_specs=[whole] * 8 + [remote],
-        out_specs=(remote, whole, whole, whole),
+        in_specs=[remote] * 8 + [whole],
+        out_specs=(remote,) * 4,
         scratch_shapes=scratch,
         compiler_params=pltpu.CompilerParams(
             collective_id=0, has_side_effects=True, vmem_limit_bytes=60 * 1024 * 1024
         ),
     )(
         unique_ids.reshape(8, 128), hash_mult.reshape(8, 128), hash_add.reshape(8, 128), lookups.T,
-        weight_in, bias_in, weight_out, bias_out.reshape(1, emb), cotangent,
+        bias_in, weight_out, bias_out.reshape(1, emb), cotangent, weight_in,
     )
     sample_out, grad_in, grad_out, grad_b_in, grad_b_out = pl.pallas_call(
         deliver,
@@ -655,15 +697,18 @@
             jax.ShapeDtypeStruct((units,), F32),
             jax.ShapeDtypeStruct((emb,), F32),
         ),
-        in_specs=[remote, remote, remote, whole],
-        out_specs=(remote, remote, remote, whole, whole),
+        in_specs=[remote] * 4,
+        out_specs=(remote,) * 5,
         scratch_shapes=[
             VMEM((samples, feats * emb), BF16),
             VMEM((8, units), F32),
             VMEM((units, emb), F32),
-            pltpu.SemaphoreType.DMA((2, 10)),
+            VMEM((16, 128), F32),
+            VMEM((units,), F32),
+            VMEM((emb,), F32),
+            pltpu.SemaphoreType.DMA((2, 12)),
         ],
-        compiler_params=pltpu.CompilerParams(vmem_limit_bytes=16 * 1024 * 1024),
+        compiler_params=pltpu.CompilerParams(vmem_limit_bytes=60 * 1024 * 1024),
     )(sample_out, grad_in, grad_out, biases)
     return sample_out, grad_in, grad_b_in, grad_out, grad_b_out
 

time: 85.1 us -> 77.9 us (0.915)
  local copies, waits for them, and re-layouts: 4.66 us -> 0 us
  Pallas kernels: 79.3 us -> 76.9 us
    unnamed x8 -> x0, local copies, waits for them, and re-layouts: 4.66 us -> none
    pallas_call x1, Pallas kernels: 4.97 us -> 3.5 us  [per_device(): pl.pallas_call(deliver, out_shape=(jax.ShapeDtypeStruct((samples, feats *...]
    pallas_call x1, Pallas kernels: 74.4 us -> 73.4 us  [per_device(): pl.pallas_call(functools.partial(kernel, dims, blocks, groups, rounds), o...]
where the time goes in v4:
time: 77.9 us; the launch traced here: 77.7 us
  Pallas kernels  76.9 us (99%)
  between operations  0.82 us (1%)
    pallas_call x1, Pallas kernels, per_device(): pl.pallas_call(functools.partial(kernel, dims, blocks, groups, rounds), o...  73.4 us
    pallas_call x1, Pallas kernels, per_device(): pl.pallas_call(deliver, out_shape=(jax.ShapeDtypeStruct((samples, feats *...  3.5 us

profile of v4, /device:TPU:1, one launch (start us, length us, event | category | flops | bytes accessed | tf_op | source)
XLA Modules:
  0.0 77.7 jit_solution(9104382268305672037)
XLA Ops:
  0.6 73.4 %shard_map.128 = (bf16[512,3328]{1,0:T(8,128)(2,1)}, f32[8,1800]{1,0:T(8,128)}, f32[1800,128]{1,0:T(8,128)}, f32[16,128]{1,0:T(8,128)}) custom-call(s32[8,128]{1,0:T(8,128)} %bitcast.6, s32[8,128]{1,0:T(8,128)} %bitcast.7, s32[8,128]{1,0:T(8,128)} %bitcast.8, s32[26,512]{1,0:T(8,128)} %bitcast.5, f32[1800]{0:T(1024)} %b_in_hbm.1, ...), custom_call_target="tpu_custom_call" | custom-call | tf_op jit(solution)/shard_map/pallas_call | solution.py:673
  74.0 3.5 %shard_map.129 = (bf16[512,3328]{1,0:T(8,128)(2,1)}, f32[8,1800]{1,0:T(8,128)}, f32[1800,128]{1,0:T(8,128)}, f32[1800]{0:T(1024)}, f32[128]{0:T(128)}) custom-call(bf16[512,3328]{1,0:T(8,128)(2,1)} %get-tuple-element.14.sample, f32[8,1800]{1,0:T(8,128)} %get-tuple-element.15.g_in, f32[1800,128]{1,0:T(8,128)} %get-tuple-element.16.g_out, ...), custom_call_target="tpu_custom_call" | custom-call | tf_op jit(solution)/shard_map/pallas_call | solution.py:691

commit v5 on v4

--- a/solution.py
+++ b/solution.py
@@ -341,21 +341,21 @@
             g_in_ref[:, first : first + valid] = summed[:, :valid]
 
     def out_send(j):
-        start, width = groups[j]
+        start, width, order = groups[j]
         at = pl.ds(start, width)
         slots[j, "ta"] = link.slot()
         link.send(slots[j, "ta"], t_send.at[:, at], t_recv.at[:, at], device(core=other))
 
     def out_first(j):
-        start, width = groups[j]
+        start, width, order = groups[j]
         at = pl.ds(start, width)
         link.copy(slots[j, "ta"], t_send.at[:, at], t_recv.at[:, at], device(core=other)).wait_recv()
         summed = (t_own[:, at] + t_recv[:, at].astype(F32)).reshape(nx, 64 // nx, width)
         t1f[:, :, at] = summed
         t1[:, :, at] = summed.astype(BF16)
-        for k, (ahead, _) in enumerate(peers("x")):
+        for k, (ahead, _) in enumerate(peers(order[0])):
             slot = slots[j, "t1", k] = link.slot()
-            link.send(slot, t1.at[ahead, :, at], t1r.at[k, :, at], device(x=ahead))
+            link.send(slot, t1.at[ahead, :, at], t1r.at[k, :, at], device(**{order[0]: ahead}))
 
     def spread_sum(j, tag, axis, ref, at, value):
         ref[here[axis], :, at] = value.astype(ref.dtype)
@@ -374,27 +374,27 @@
         return total([ref[k, :, at].astype(F32) for k in range(size[axis])])
 
     def out_second(j):
-        start, width = groups[j]
-        at = pl.ds(start, width)
-        for k, (ahead, _) in enumerate(peers("x")):
-            link.copy(slots[j, "t1", k], t1.at[ahead, :, at], t1r.at[k, :, at], device(x=ahead)).wait_recv()
-        summed = total([t1f[x, :, at]] + [t1r[k, :, at].astype(F32) for k in range(nx - 1)])
-        spread_sum(j, "t2", "y", t2, at, summed)
+        start, width, order = groups[j]
+        at = pl.ds(start, width)
+        for k, (ahead, _) in enumerate(peers(order[0])):
+            link.copy(slots[j, "t1", k], t1.at[ahead, :, at], t1r.at[k, :, at], device(**{order[0]: ahead})).wait_recv()
+        summed = total([t1f[here[order[0]], :, at]] + [t1r[k, :, at].astype(F32) for k in range(size[order[0]] - 1)])
+        spread_sum(j, "t2", order[1], t2, at, summed)
 
     def out_third(j):
-        start, width = groups[j]
-        at = pl.ds(start, width)
-        spread_sum(j, "t3", "z", t3, at, spread_total(j, "t2", "y", t2, at))
+        start, width, order = groups[j]
+        at = pl.ds(start, width)
+        spread_sum(j, "t3", order[2], t3, at, spread_total(j, "t2", order[1], t2, at))
 
     def out_fourth(j):
-        start, width = groups[j]
-        at = pl.ds(start, width)
-        spread_sum(j, "t4", "x", tf.at[core], at, spread_total(j, "t3", "z", t3, at))
+        start, width, order = groups[j]
+        at = pl.ds(start, width)
+        spread_sum(j, "t4", order[0], tf.at[core], at, spread_total(j, "t3", order[2], t3, at))
 
     def out_fifth(j):
-        start, width = groups[j]
-        at = pl.ds(start, width)
-        spread_wait(j, "t4", "x", tf.at[core], at)
+        start, width, order = groups[j]
+        at = pl.ds(start, width)
+        spread_wait(j, "t4", order[0], tf.at[core], at)
         slot = slots[j, "t5"] = link.slot()
         ref = tf.at[core, :, :, at]
         link.send(slot, ref, ref, device(core=other))
@@ -407,15 +407,15 @@
         result_copies.append(made)
 
     def out_last(j):
-        start, width = groups[j]
+        start, width, order = groups[j]
         at = pl.ds(start, width)
         ref = tf.at[other, :, :, at]
         link.copy(slots[j, "t5"], ref, ref, device(core=other)).wait_recv()
         for first in range(start, start + width, 128):
             valid = min(128, units - first)
-            part = tf[:, :, :, first : first + 128].reshape(128, 128)
+            part = tf[:, :, :, first : first + 128].astype(F32).reshape(128, 128)
             g_out_ref[first : first + valid, :] = jnp.transpose(part)[:valid, :]
-        deliver_rows(start, min(width, units - start), 8 + j)
+        deliver_rows(start, min(width, units - start), 13 + j)
 
     def bias_first():
         slots["b", "c"] = link.slot()
@@ -436,7 +436,7 @@
 
     def bias_last():
         bias_ref[...] = spread_total("b", "z", "z", bz, everything)
-        made = pltpu.make_async_copy(bias_ref, bias_hbm, out_sems.at[11])
+        made = pltpu.make_async_copy(bias_ref, bias_hbm, out_sems.at[9])
         made.start()
         result_copies.append(made)
 
@@ -448,7 +448,8 @@
         (2, 1): [(in_second, 0)],
         (3, 0): [(in_first, 2), (out_first, 1), (out_second, 0), (in_third, 0)],
         (3, 1): [(in_second, 1)],
-        (4, 3): [(in_first, 3), (out_first, 2), (bias_second,), (out_second, 1), (out_third, 0), (in_last, 0)],
+        (4, 1): [(in_first, 3), (out_first, 2), (bias_second,)],
+        (4, 4): [(out_second, 1), (out_third, 0), (in_last, 0)],
         (4, 7): [(in_second, 2), (in_third, 1)],
         (4, 12): [(out_second, 2), (bias_third,), (out_third, 1), (out_fourth, 0)],
         (4, 14): [(in_second, 3)],
@@ -492,7 +493,7 @@
         grad = jnp.dot(demb_t[...], hidden[:, :width], preferred_element_type=F32)
         t_own[:, at] = jnp.where(core == 0, grad[:64], grad[64:])
         t_send[:, at] = jnp.where(core == 0, grad[64:], grad[:64]).astype(BF16)
-        for g, (first, wide) in enumerate(groups):
+        for g, (first, wide, _) in enumerate(groups):
             if start + width == first + wide:
                 out_send(g)
         rows_half = codes // 2
@@ -540,7 +541,7 @@
         look_up(cuts[i], cuts[i + 1], i)
         advance(4, cuts[i + 1])
     assert not points
-    made = pltpu.make_async_copy(g_in_ref, g_in_hbm, out_sems.at[7])
+    made = pltpu.make_async_copy(g_in_ref, g_in_hbm, out_sems.at[12])
     made.start()
     result_copies.append(made)
     link.finish()
@@ -598,7 +599,7 @@
             first += each
         blocks.append((start, width, stripes))
         start += width
-    groups = [(0, 1024), (1024, 512), (1536, padded - 1536)]
+    groups = [(0, 1024, "xyz"), (1024, 512, "xyz"), (1536, padded - 1536, "xyz")]
     rounds = [
         (0, 384, (("xyz", 0, 128), ("yzx", 128, 128), ("zxy", 256, 128))),
         (768, 640, (("xyz", 0, 256), ("yzx", 256, 256), ("zxy", 512, 128))),
@@ -658,7 +659,7 @@
         VMEM((3, 64 // nx, padded), BF16),
         VMEM((ny, 64 // nx, padded), BF16),
         VMEM((nz, 64 // nx, padded), BF16),
-        VMEM((2, nx, 64 // nx, padded), F32),
+        VMEM((2, nx, 64 // nx, padded), BF16),
         VMEM((2, 16, 128), F32),
         VMEM((nx, 16, 128), F32),
         VMEM((ny, 16, 128), F32),
@@ -666,7 +667,7 @@
         pltpu.SemaphoreType.DMA((260,)),
         pltpu.SemaphoreType.DMA((260,)),
         pltpu.SemaphoreType.DMA((8,)),
-        pltpu.SemaphoreType.DMA((12,)),
+        pltpu.SemaphoreType.DMA((16,)),
     ]
     whole = pl.BlockSpec(memory_space=pltpu.VMEM)
     remote = pl.BlockSpec(memory_space=pl.ANY)

time: 77.9 us -> 77.3 us (level)
  no operation moved by 1% of the time
where the time goes in v5:
time: 77.3 us; the launch traced here: 77.1 us
  Pallas kernels  76.3 us (99%)
  between operations  0.82 us (1%)
    pallas_call x1, Pallas kernels, per_device(): pl.pallas_call(functools.partial(kernel, dims, blocks, groups, rounds), o...  72.8 us
    pallas_call x1, Pallas kernels, per_device(): pl.pallas_call(deliver, out_shape=(jax.ShapeDtypeStruct((samples, feats *...  3.5 us

profile of v5, /device:TPU:1, one launch (start us, length us, event | category | flops | bytes accessed | tf_op | source)
XLA Modules:
  0.0 77.1 jit_solution(2376704466641674673)
XLA Ops:
  0.6 72.8 %shard_map.128 = (bf16[512,3328]{1,0:T(8,128)(2,1)}, f32[8,1800]{1,0:T(8,128)}, f32[1800,128]{1,0:T(8,128)}, f32[16,128]{1,0:T(8,128)}) custom-call(s32[8,128]{1,0:T(8,128)} %bitcast.6, s32[8,128]{1,0:T(8,128)} %bitcast.7, s32[8,128]{1,0:T(8,128)} %bitcast.8, s32[26,512]{1,0:T(8,128)} %bitcast.5, f32[1800]{0:T(1024)} %b_in_hbm.1, ...), custom_call_target="tpu_custom_call" | custom-call | tf_op jit(solution)/shard_map/pallas_call | solution.py:674
  73.4 3.5 %shard_map.129 = (bf16[512,3328]{1,0:T(8,128)(2,1)}, f32[8,1800]{1,0:T(8,128)}, f32[1800,128]{1,0:T(8,128)}, f32[1800]{0:T(1024)}, f32[128]{0:T(128)}) custom-call(bf16[512,3328]{1,0:T(8,128)(2,1)} %get-tuple-element.14.sample, f32[8,1800]{1,0:T(8,128)} %get-tuple-element.15.g_in, f32[1800,128]{1,0:T(8,128)} %get-tuple-element.16.g_out, ...), custom_call_target="tpu_custom_call" | custom-call | tf_op jit(solution)/shard_map/pallas_call | solution.py:692
